TPU v7x, 32 devices: a whole 2x2x4 slice. The times are simulated.
32 devices in a mesh: member: 2 (over y), gx: 16 (over z, x, core).
Axes of the slice: x: 2, y: 2, z: 4, core: 2. Of those that a mesh axis runs over, the one named last changes fastest.
Arguments:
- inputs: float32 [32768, 557], P(('member', 'gx')), parts along dimension 0, may hold values from -6 to 6
- tracer: float32 [60, 256, 128], P(None, ('member', 'gx')), parts along dimension 1, may hold values from -6 to 6
- speed_along: float32 [256, 128], P(('member', 'gx')), parts along dimension 0, may hold values from -0.5 to 0.5
- speed_across: float32 [256, 128], P(('member', 'gx')), parts along dimension 0, may hold values from -0.3 to 0.3
- inverse_list: int32 [32768], P(('member', 'gx')), parts along dimension 0, may hold values from -1 to 1023, as said below
- weight_one: float32 [557, 768], replicated, may hold values from -0.25 to 0.25
- bias_one: float32 [768], replicated, may hold values from -3 to 3
- weight_two: float32 [768, 640], replicated, may hold values from -0.3125 to 0.3125
- bias_two: float32 [640], replicated, may hold values from -3 to 3
- weight_three: float32 [640, 512], replicated, may hold values from -0.3125 to 0.3125
- bias_three: float32 [512], replicated, may hold values from -3 to 3
- weight_four: float32 [512, 640], replicated, may hold values from -0.375 to 0.375
- bias_four: float32 [640], replicated, may hold values from -3 to 3
- weight_five: float32 [640, 640], replicated, may hold values from -0.3125 to 0.3125
- bias_five: float32 [640], replicated, may hold values from -3 to 3
- weight_six: float32 [640, 368], replicated, may hold values from -0.3125 to 0.3125
- bias_six: float32 [368], replicated, may hold values from -3 to 3
Outputs:
- tendencies: float32 [32768, 368], P(('member', 'gx')), parts along dimension 0
- advected: float32 [60, 256, 128], P(None, ('member', 'gx')), parts along dimension 1
There are 2 independent parts, one for each index of `member`. A program takes and returns all parts, laid end to end along the dimension named above; an argument that names none is the same for every part. Nothing has to cross between parts.
Inputs may be any that keep to these rules, and one draw needn't show every extreme that they name: `inverse_list`: no two day columns of one tile share a slot position. Every tile evaluates exactly 512 day columns in all, and half of all columns are day columns. Some tile's columns are all day; such a tile fills all 64 slots to every tile.
All inputs are finite; a program needn't handle non-finite values.
Results may differ from a plain program's by a relative error of at most 0.0003.
Values sent between devices are 32-bit elements; how exact they have to be, the bound alone decides.
No kernel may reach another device: no remote copies, remote signals or barrier semaphores. Data moves between devices by JAX's collectives and lax.ppermute only.
A program may use at most 64 MiB of HBM per device.

v0:
```python
import functools
import jax
import jax.numpy as jnp
from jax import lax
from jax.experimental import pallas as pl
from jax.experimental.pallas import tpu as pltpu
from jax.sharding import PartitionSpec as P

F32, BF16, F8 = jnp.float32, jnp.bfloat16, jnp.float8_e4m3fn
LANES = 128
CHUNK = 512
HALO = 6
GROUP = 32
WEIGHT_MAX = (0.25, 0.3125, 0.3125, 0.375, 0.3125, 0.3125)
BIAS_MAX = 3.0
INPUT_MAX = 6.0
SILU_DIP = 0.28
TOP = 440.0
WEIGHT_STEP = 2.0**10
LOW_STEP = 2.0**8
NETWORK_VMEM = 60_000_000
ADVECT_VMEM = 8 * 2**20


def round_up(value, unit):
    return -(-value // unit) * unit


def network_kernel(*refs, sizes, levels, axis):
    small_hbm, x_hbm, weights_hbm, refs = refs[:10], refs[10], refs[11:17], refs[17:]
    (tend_hbm, field_hbm, pay_a, pay_b), refs = refs[:4], refs[4:]
    x_in, weights_in, refs = refs[0], refs[1:7], refs[7:]
    cats, cats8, columns, refs = refs[:6], refs[6:12], refs[12:18], refs[18:]
    inverse, tracer, along, across, *biases = refs[:10]
    holds, holds8, refs = refs[10:12], refs[12:14], refs[14:]
    w_tail, x_tail, b_six, tend, peaks, shrinks, field, *sems = refs
    x_sems, w_sems, out_sems, small_sems, field_sems = sems

    chunks = x_hbm.shape[1] // CHUNK
    rows, levels_wide = field.shape[0], field.shape[1]
    depth_in = sizes[0]
    aligned = depth_in // 8 * 8
    whole = depth_in // LANES * LANES
    padded = [cats[layer].shape[1] for layer in range(6)]

    def x_copy(c):
        part = pl.ds(c * CHUNK, CHUNK)
        return pltpu.make_async_copy(x_hbm.at[:, part], x_in.at[:, part], x_sems.at[c])

    def w_copy(layer):
        target = weights_in[layer]
        if layer == 5:
            target = target.at[pl.ds(0, sizes[6])]
        return pltpu.make_async_copy(weights_hbm[layer], target, w_sems.at[layer])

    def small_copy(i):
        target = (inverse, tracer, along, across, *biases)[i]
        return pltpu.make_async_copy(small_hbm[i], target, small_sems.at[i])

    def out_copy(c):
        part = pl.ds(c * CHUNK, CHUNK)
        return pltpu.make_async_copy(
            tend.at[:, part], tend_hbm.at[:, part], out_sems.at[c]
        )

    def bias_columns(layer):
        count = sizes[layer + 1]
        source = biases[layer]
        if count % LANES:
            b_six[0:1, :] = jnp.zeros((1, b_six.shape[1]), F32)
            b_six[0:1, 0:count] = source[...].reshape(1, count)
            row = b_six[0:1, :]
        else:
            row = source[...].reshape(1, count)
        scale = 0.5 if layer < 5 else 1.0
        for n in range(0, count, LANES):
            block = jnp.broadcast_to(row[:, n : n + LANES], (LANES, LANES)).T * scale
            columns[layer][n : n + LANES, :] = block

    def put_weights(layer, lines, k, block):
        depth = padded[layer]
        if layer < 5:
            block = block * 0.5
        high = block.astype(BF16)
        low = block - high.astype(F32)
        step = WEIGHT_STEP * (2.0 if layer < 5 else 1.0)
        lanes, far = slice(k, k + LANES), slice(depth + k, depth + k + LANES)
        cats[layer][lines, lanes] = high
        cats8[layer][lines, lanes] = (block * step).astype(F8)
        cats8[layer][lines, far] = (low * (step * LOW_STEP)).astype(F8)

    def prepare(layer, part, parts):
        work = [
            (n, k)
            for n in range(0, round_up(sizes[layer + 1], LANES), LANES)
            for k in range(0, padded[layer], LANES)
        ]
        for n, k in work[part * len(work) // parts : (part + 1) * len(work) // parts]:
            lines, lanes = slice(n, n + LANES), slice(k, k + LANES)
            if layer == 5:
                block = weights_in[5][lines, lanes]
            elif layer == 0 and k >= whole:
                block = w_tail[:, lines].T
            else:
                block = weights_in[layer][lanes, lines].T
            put_weights(layer, lines, k, block)

    def put_rows(layer, start, cols, value, scale):
        depth = padded[layer]
        high = value.astype(BF16)
        low = value - high.astype(F32)
        size = value.shape[0]
        holds[layer % 2][start : start + size, cols] = high
        hold8 = holds8[layer % 2]
        hold8[start : start + size, cols] = (low * (scale * LOW_STEP)).astype(F8)
        hold8[depth + start : depth + start + size, cols] = (value * scale).astype(F8)

    def prepare_inputs(c):
        cols = slice(c * CHUNK, (c + 1) * CHUNK)
        x_tail[0 : aligned - whole, cols] = x_in[whole:aligned, cols]
        x_tail[aligned - whole : depth_in - whole, cols] = x_in[aligned:depth_in, cols]
        for k in range(0, whole, LANES):
            put_rows(0, k, cols, x_in[k : k + LANES, cols], TOP / INPUT_MAX)
        put_rows(0, whole, cols, x_tail[:, cols], TOP / INPUT_MAX)

    def product(layer, c):
        depth = padded[layer]
        cols = slice(c * CHUNK, (c + 1) * CHUNK)
        main = jnp.dot(
            cats[layer][...],
            holds[layer % 2][0:depth, cols],
            preferred_element_type=F32,
        )
        rest = jnp.dot(
            cats8[layer][...],
            holds8[layer % 2][0 : 2 * depth, cols],
            preferred_element_type=F32,
        )
        return main, rest

    def finish(layer, c, main, rest):
        cols = slice(c * CHUNK, (c + 1) * CHUNK)
        unit = 1.0 / (WEIGHT_STEP * LOW_STEP * (2.0 if layer < 5 else 1.0))
        if layer == 0:
            shrink, peak = jnp.full((1, CHUNK), INPUT_MAX / TOP, F32), INPUT_MAX
        else:
            shrink, peak = shrinks[layer : layer + 1, cols], peaks[layer : layer + 1, cols]
        bias = columns[layer][...]
        value = main + rest * (shrink * unit)
        value = value + jnp.concatenate([bias] * (CHUNK // LANES), axis=1)
        if layer < 5:
            value = value + value * jnp.tanh(value)
            limit = (sizes[layer] * WEIGHT_MAX[layer]) * peak + BIAS_MAX
            limit = jnp.broadcast_to(jnp.asarray(limit, F32), (1, CHUNK))
            put_rows(layer + 1, 0, cols, value, TOP / limit)
            shrinks[layer + 1 : layer + 2, cols] = limit / TOP
            highest = jnp.max(value, axis=0, keepdims=True)
            peaks[layer + 1 : layer + 2, cols] = jnp.maximum(highest, SILU_DIP)
            return
        for part in range(CHUNK // LANES):
            r = c * (CHUNK // LANES) + part
            day = inverse[r : r + 1, :] >= 0
            shown = jnp.where(
                day, value[: sizes[6], part * LANES : (part + 1) * LANES], 0.0
            )
            tend[:, r * LANES : (r + 1) * LANES] = shown
            field[r, 0:levels, :] = (
                tracer[pl.ds(r, levels, stride=rows), :] + shown[0:levels]
            )
        out_copy(c).start()

    w_copy(0).start()
    for c in range(chunks):
        x_copy(c).start()
    for i in range(10):
        small_copy(i).start()
    w_copy(1).start()
    w_tail[...] = jnp.zeros(w_tail.shape, F32)
    x_tail[...] = jnp.zeros(x_tail.shape, F32)
    weights_in[5][sizes[6] :, :] = jnp.zeros(
        (weights_in[5].shape[0] - sizes[6], sizes[5]), F32
    )
    w_copy(0).wait()
    w_tail[0 : aligned - whole, :] = weights_in[0][whole:aligned, :]
    w_tail[aligned - whole : depth_in - whole, :] = weights_in[0][aligned:depth_in, :]
    prepare(0, 0, 1)
    for layer in range(2, 6):
        w_copy(layer).start()
    x_copy(0).wait()
    prepare_inputs(0)

    for layer in range(6):
        if 0 < layer < 5:
            w_copy(layer + 1).wait()
        for c in range(chunks):
            main, rest = product(layer, c)
            if layer == 0 and c == 0:
                for i in range(10):
                    small_copy(i).wait()
                bias_columns(0)
                for i in range(1, chunks):
                    x_copy(i).wait()
                    prepare_inputs(i)
                w_copy(1).wait()
            if layer < 5:
                prepare(layer + 1, c, chunks)
                if c == chunks - 1:
                    bias_columns(layer + 1)
            if layer == 4 and c == 0:
                for r in range(rows):
                    field[r, levels : levels + 1, :] = along[r : r + 1, :]
                    field[r, levels + 1 : levels + 2, :] = across[r : r + 1, :]
                    field[r, levels + 2 : levels_wide, :] = jnp.zeros(
                        (levels_wide - levels - 2, LANES), F32
                    )
            finish(layer, c, main, rest)

    odd = lax.rem(lax.axis_index(axis), 2)
    leaving = [
        pltpu.make_async_copy(
            field.at[pl.ds((rows - HALO) * odd, HALO)], pay_a, field_sems.at[0]
        ),
        pltpu.make_async_copy(
            field.at[pl.ds((rows - HALO) * (1 - odd), HALO)], pay_b, field_sems.at[1]
        ),
        pltpu.make_async_copy(field, field_hbm, field_sems.at[2]),
    ]
    for copy in leaving:
        copy.start()
    for copy in leaving:
        copy.wait()
    for c in range(chunks):
        out_copy(c).wait()


def network(inverse, tracer, along, across, biases, x, weights, axis):
    sizes = [x.shape[0]] + [b.shape[0] for b in biases]
    width = x.shape[1]
    rows = along.shape[0]
    levels = tracer.shape[0] // rows
    levels_wide = round_up(levels + 2, 8)
    chunks = width // CHUNK
    padded = [round_up(s, LANES) for s in sizes]
    deepest = max(padded[:6])
    tail = padded[0] - sizes[0] // LANES * LANES
    hbm = pl.BlockSpec(memory_space=pl.ANY)
    total = sum(sizes[i] * sizes[i + 1] for i in range(6)) * width
    return pl.pallas_call(
        functools.partial(network_kernel, sizes=sizes, levels=levels, axis=axis),
        out_shape=(
            jax.ShapeDtypeStruct((sizes[6], width), F32),
            jax.ShapeDtypeStruct((rows, levels_wide, LANES), F32),
            jax.ShapeDtypeStruct((HALO, levels_wide, LANES), F32),
            jax.ShapeDtypeStruct((HALO, levels_wide, LANES), F32),
        ),
        in_specs=[hbm] * 17,
        out_specs=(hbm,) * 4,
        scratch_shapes=[
            pltpu.VMEM(x.shape, F32),
            *[pltpu.VMEM(w.shape, F32) for w in weights[:5]],
            pltpu.VMEM((padded[6], sizes[5]), F32),
            *[pltpu.VMEM((padded[i + 1], padded[i]), BF16) for i in range(6)],
            *[pltpu.VMEM((padded[i + 1], 2 * padded[i]), F8) for i in range(6)],
            *[pltpu.VMEM((padded[i + 1], LANES), F32) for i in range(6)],
            pltpu.VMEM(inverse.shape, jnp.int32),
            pltpu.VMEM(tracer.shape, F32),
            pltpu.VMEM(along.shape, F32),
            pltpu.VMEM(across.shape, F32),
            *[pltpu.VMEM(b.shape, F32) for b in biases],
            *[pltpu.VMEM((deepest, width), BF16)] * 2,
            *[pltpu.VMEM((2 * deepest, width), F8)] * 2,
            pltpu.VMEM((tail, sizes[1]), F32),
            pltpu.VMEM((tail, width), F32),
            pltpu.VMEM((8, padded[6]), F32),
            pltpu.VMEM((sizes[6], width), F32),
            pltpu.VMEM((8, width), F32),
            pltpu.VMEM((8, width), F32),
            pltpu.VMEM((rows, levels_wide, LANES), F32),
            pltpu.SemaphoreType.DMA((chunks,)),
            pltpu.SemaphoreType.DMA((6,)),
            pltpu.SemaphoreType.DMA((chunks,)),
            pltpu.SemaphoreType.DMA((10,)),
            pltpu.SemaphoreType.DMA((3,)),
        ],
        compiler_params=pltpu.CompilerParams(vmem_limit_bytes=NETWORK_VMEM),
        cost_estimate=pl.CostEstimate(
            flops=4 * total, bytes_accessed=14_000_000, transcendentals=3_000_000
        ),
        name="column_network",
    )(inverse, tracer, along, across, *biases, x, *weights)


def half_minmod(first, second):
    return 0.5 * (
        jnp.maximum(jnp.minimum(first, second), 0.0)
        + jnp.minimum(jnp.maximum(first, second), 0.0)
    )


def cat(values):
    return values[0] if len(values) == 1 else jnp.concatenate(values, axis=0)


def advect_kernel(field, got_a, got_b, out, wide, speeds, sem, *, levels, axis):
    rows = field.shape[0]
    odd = lax.rem(lax.axis_index(axis), 2)
    own = pltpu.make_async_copy(field, wide.at[pl.ds(HALO, rows)], sem)
    own.start()
    wide[pl.ds((HALO + rows) * odd, HALO)] = got_a[...]
    wide[pl.ds((HALO + rows) * (1 - odd), HALO)] = got_b[...]

    def place(i):
        for kind in range(2):
            courant = jnp.broadcast_to(
                wide[i, levels + kind : levels + kind + 1, :], (8, LANES)
            )
            speeds[2 * kind, i] = jnp.maximum(courant, 0.0)
            speeds[2 * kind + 1, i] = jnp.minimum(courant, 0.0)

    for i in range(HALO):
        place(i)
        place(HALO + rows + i)
    own.wait()
    for i in range(HALO, HALO + rows):
        place(i)
    groups = wide.shape[1] // GROUP

    def group(g, carry):
        wavefront(g, groups, levels, out, wide, speeds, rows)
        return carry

    lax.fori_loop(0, groups, group, 0)


def wavefront(g, groups, levels, out, wide, speeds, rows):
    base = pl.multiple_of(g * GROUP, GROUP)
    blocks = GROUP // 8
    keep = levels - (groups - 1) * GROUP
    fields = [{}, {}, {}]
    steps, slopes, fluxes = [{}, {}, {}], [{}, {}, {}], [{}, {}, {}]
    reach = [(-4, rows + 3), (-2, rows + 1), (0, rows - 1)]
    shape = (blocks, 8, LANES)

    def load(i):
        return wide[i + HALO, pl.ds(base, GROUP), :].reshape(shape)

    def courant(kind, at):
        return cat([jnp.broadcast_to(speeds[kind, i + HALO], shape) for i in at])

    def pieces(value, count):
        return [value[n * blocks : (n + 1) * blocks] for n in range(count)]

    def face(active, at):
        ahead, behind = courant(0, at), courant(1, at)
        upper = cat([fields[k][i] - slopes[k][i] for k, i in zip(active, at)])
        lower = cat([fields[k][i - 1] + slopes[k][i - 1] for k, i in zip(active, at)])
        return ahead * lower + behind * upper

    rest = []
    for i in range(-HALO, -2):
        fields[0][i] = load(i)
    for t in range(-4, rows + 6):
        active = [k for k in range(3) if reach[k][0] <= t - 3 * k <= reach[k][1]]
        if t + 2 < rows + HALO:
            fields[0][t + 2] = load(t + 2)
        for k in active:
            c = t - 3 * k
            if c == reach[k][0]:
                f = fields[k]
                for i in (c - 1, c, c + 1):
                    steps[k][i] = f[i] - f[i - 1]
                for i in (c - 1, c):
                    slopes[k][i] = half_minmod(steps[k][i + 1], steps[k][i])
                fluxes[k][c] = face([k], [c])
        at = [t - 3 * k for k in active]
        here = cat([fields[k][i] for k, i in zip(active, at)])
        back = here - pltpu.roll(here, 1, 2)
        new = cat(
            [fields[k][i + 2] - fields[k][i + 1] for k, i in zip(active, at)]
        )
        last = cat([steps[k][i + 1] for k, i in zip(active, at)])
        bend = half_minmod(pltpu.roll(back, LANES - 1, 2), back)
        slope = half_minmod(new, last)
        for k, i, a_step, a_slope in zip(
            active, at, pieces(new, len(at)), pieces(slope, len(at))
        ):
            steps[k][i + 2], slopes[k][i + 1] = a_step, a_slope
        side = courant(2, at) * pltpu.roll(here + bend, 1, 2)
        side = side + courant(3, at) * (here - bend)
        flux = face(active, [i + 1 for i in at])
        for k, i, a_flux in zip(active, at, pieces(flux, len(at))):
            fluxes[k][i + 1] = a_flux
        moved = cat([fluxes[k][i] for k, i in zip(active, at)]) - flux
        moved = here + (moved + (side - pltpu.roll(side, LANES - 1, 2)))
        for k, i, value in zip(active, at, pieces(moved, len(at))):
            if k == 0:
                fields[1][i] = value
            elif k == 1:
                fields[2][i] = 0.75 * fields[0][i] + 0.25 * value
            else:
                value = 1.0 / 3.0 * fields[0][i] + 2.0 / 3.0 * value
                value = value.reshape(GROUP, LANES)
                out[pl.ds(base * rows + i, keep, stride=rows), :] = value[:keep]
                rest.append((i, value[keep:]))
    if keep < GROUP:

        @pl.when(g < groups - 1)
        def _():
            for i, value in rest:
                lines = pl.ds((base + keep) * rows + i, GROUP - keep, stride=rows)
                out[lines, :] = value


def advect(field, got_a, got_b, levels, axis):
    rows, levels_wide, across = field.shape
    vmem = pl.BlockSpec(memory_space=pltpu.VMEM)
    return pl.pallas_call(
        functools.partial(advect_kernel, levels=levels, axis=axis),
        out_shape=jax.ShapeDtypeStruct((levels * rows, across), F32),
        in_specs=[pl.BlockSpec(memory_space=pl.ANY), vmem, vmem],
        out_specs=vmem,
        scratch_shapes=[
            pltpu.VMEM((rows + 2 * HALO, levels_wide, across), F32),
            pltpu.VMEM((4, rows + 2 * HALO, 8, across), F32),
            pltpu.SemaphoreType.DMA,
        ],
        compiler_params=pltpu.CompilerParams(vmem_limit_bytes=ADVECT_VMEM),
        name="advect_sections",
    )(field, got_a, got_b)


def shards(inputs, tracer, speed_along, speed_across, inverse_list, *params):
    weights, biases = list(params[0::2]), params[1::2]
    weights[5] = weights[5].T
    levels, rows, across = tracer.shape
    tendencies, field, pay_a, pay_b = network(
        inverse_list.reshape(rows, across),
        tracer.reshape(levels * rows, across),
        speed_along,
        speed_across,
        biases,
        inputs.T,
        weights,
        "gx",
    )
    count = lax.axis_size("gx")
    outer = [(i, (i - 1 if i % 2 == 0 else i + 1) % count) for i in range(count)]
    inner = [(i, i + 1 if i % 2 == 0 else i - 1) for i in range(count)]
    got_a = lax.ppermute(pay_a, "gx", outer)
    got_b = lax.ppermute(pay_b, "gx", inner)
    advected = advect(field, got_a, got_b, levels, "gx")
    return tendencies.T, advected.reshape(levels, rows, across)


def solution(mesh):
    placed = (
        P(("member", "gx"), None),
        P(None, ("member", "gx"), None),
        P(("member", "gx"), None),
        P(("member", "gx"), None),
        P(("member", "gx")),
        *[P()] * 12,
    )
    return jax.shard_map(
        shards,
        mesh=mesh,
        in_specs=placed,
        out_specs=(P(("member", "gx"), None), P(None, ("member", "gx"), None)),
        check_vma=False,
    )
```

profile of v0, /device:TPU:0, one launch (start us, length us, event | category | flops | bytes accessed | tf_op | source)
XLA Modules:
  0.0 33.2 jit_solution(14592099366238515144)
XLA Ops:
  0.6 19.2 %column_network.1 = (f32[368,1024]{1,0:T(8,128)}, f32[8,64,128]{2,1,0:T(8,128)}, f32[6,64,128]{2,1,0:T(8,128)}, f32[6,64,128]{2,1,0:T(8,128)}) custom-call(s32[8,128]{1,0:T(8,128)} %bitcast.10, f32[480,128]{1,0:T(8,128)} %bitcast.9, f32[8,128]{1,0:T(8,128)} %refs_2_.1, f32[8,128]{1,0:T(8,128)} %refs_3_.1, f32[768]{0:T(1024)} %refs_4_.1, f32[640]{0:T(1024)} %refs_5_.1, ...), custom_call_target="tpu_custom_call" | custom-call | flops 9092202496 | bytes 14000000 | tf_op jit(solution)/shard_map/column_network/pallas_call | solution.py:248
  19.8 5.5 %collective-permute-start = (f32[6,64,128]{2,1,0:T(8,128)}, f32[6,64,128]{2,1,0:T(8,128)S(1)}, u32[]{:S(2)}, u32[]{:S(2)}) collective-permute-start(f32[6,64,128]{2,1,0:T(8,128)} %get-tuple-element.8), channel_id=1, source_target_pairs={{0,15},{1,2},{2,1},{3,4},{4,3},{5,6},{6,5},{7,8},{8,7},{9,10},{10,... | collective-permute-start | bytes 589832 | tf_op jit(solution)/shard_map/ppermute | solution.py:449
  25.3 0.0 collective-permute-start.1
  25.3 3.6 %collective-permute-done.got_a = f32[6,64,128]{2,1,0:T(8,128)S(1)} collective-permute-done((f32[6,64,128]{2,1,0:T(8,128)}, f32[6,64,128]{2,1,0:T(8,128)S(1)}, u32[]{:S(2)}, u32[]{:S(2)}) %collective-permute-start) | collective-permute-done | bytes 196640 | tf_op jit(solution)/shard_map/ppermute | solution.py:449
  28.9 0.0 collective-permute-done.1.got_b
  28.9 0.0 copy-start
  28.9 0.9 %copy-done = f32[8,64,128]{2,1,0:T(8,128)S(1)} copy-done((f32[8,64,128]{2,1,0:T(8,128)S(1)}, f32[8,64,128]{2,1,0:T(8,128)}, u32[]{:S(2)}) %copy-start) | copy-done | bytes 262168
  29.8 3.2 %advect_sections.1 = f32[480,128]{1,0:T(8,128)} custom-call(f32[8,64,128]{2,1,0:T(8,128)S(1)} %copy-done, f32[6,64,128]{2,1,0:T(8,128)S(1)} %collective-permute-done.got_a, f32[6,64,128]{2,1,0:T(8,128)S(1)} %collective-permute-done.1.got_b), custom_call_target="tpu_custom_call" | custom-call | tf_op jit(solution)/shard_map/advect_sections/pallas_call | solution.py:417
Async XLA Ops:
  19.8 9.1 %collective-permute-start = (f32[6,64,128]{2,1,0:T(8,128)}, f32[6,64,128]{2,1,0:T(8,128)S(1)}, u32[]{:S(2)}, u32[]{:S(2)}) collective-permute-start(f32[6,64,128]{2,1,0:T(8,128)} %get-tuple-element.8), channel_id=1, source_target_pairs={{0,15},{1,2},{2,1},{3,4},{4,3},{5,6},{6,5},{7,8},{8,7},{9,10},{10,... | collective-permute-start | bytes 589832 | tf_op jit(solution)/shard_map/ppermute | solution.py:449
  25.3 3.6 %collective-permute-start.1 = (f32[6,64,128]{2,1,0:T(8,128)}, f32[6,64,128]{2,1,0:T(8,128)S(1)}, u32[]{:S(2)}, u32[]{:S(2)}) collective-permute-start(f32[6,64,128]{2,1,0:T(8,128)} %get-tuple-element.9), channel_id=1, source_target_pairs={{0,1},{1,0},{2,3},{3,2},{4,5},{5,4},{6,7},{7,6},{8,9},{9,8},{10,11... | collective-permute-start | bytes 589832 | tf_op jit(solution)/shard_map/ppermute | solution.py:450
  28.9 1.0 %copy-start = (f32[8,64,128]{2,1,0:T(8,128)S(1)}, f32[8,64,128]{2,1,0:T(8,128)}, u32[]{:S(2)}) copy-start(f32[8,64,128]{2,1,0:T(8,128)} %get-tuple-element.7.field) | copy-start | bytes 786436
where the time goes:
time: 33.3 us; the launch traced here: 33.2 us
  Pallas kernels  22.4 us (67%)
  starting transfers between devices  5.49 us (16%)
  waiting for transfers between devices  3.56 us (11%)
  local copies, waits for them, and re-layouts  0.95 us (3%)
  between operations  0.81 us (2%)
    pallas_call x1, Pallas kernels, network(): pl.pallas_call(functools.partial(network_kernel, sizes=sizes, levels=leve...  19.2 us
    ppermute x1, starting transfers between devices, shards(): got_a = lax.ppermute(pay_a, 'gx', outer)  5.48 us
    ppermute x1, waiting for transfers between devices, shards(): got_a = lax.ppermute(pay_a, 'gx', outer)  3.56 us
    pallas_call x1, Pallas kernels, advect(): pl.pallas_call(functools.partial(advect_kernel, levels=levels, axis=axis)...  3.17 us
    unnamed x2, local copies, waits for them, and re-layouts  0.95 us
  transfers between devices with their start and end apart: 2, of which 1 were waited for; matrix products, arithmetic and copies ran while one was open for 0% of the time, Pallas kernels for 0%

commit v1 on v0

--- a/solution.py
+++ b/solution.py
@@ -11,6 +11,7 @@
 CHUNK = 512
 HALO = 6
 GROUP = 32
+FIRST = 256
 WEIGHT_MAX = (0.25, 0.3125, 0.3125, 0.375, 0.3125, 0.3125)
 BIAS_MAX = 3.0
 INPUT_MAX = 6.0
@@ -19,7 +20,8 @@
 WEIGHT_STEP = 2.0**10
 LOW_STEP = 2.0**8
 NETWORK_VMEM = 60_000_000
-ADVECT_VMEM = 8 * 2**20
+ADVECT_VMEM = 54_000_000
+ROOM = 128
 
 
 def round_up(value, unit):
@@ -34,18 +36,24 @@
     inverse, tracer, along, across, *biases = refs[:10]
     holds, holds8, refs = refs[10:12], refs[12:14], refs[14:]
     w_tail, x_tail, b_six, tend, peaks, shrinks, field, *sems = refs
-    x_sems, w_sems, out_sems, small_sems, field_sems = sems
+    x_sems, w_sems, out_sems, small_sems, field_sems, first_sems = sems
 
     chunks = x_hbm.shape[1] // CHUNK
     rows, levels_wide = field.shape[0], field.shape[1]
     depth_in = sizes[0]
     aligned = depth_in // 8 * 8
     whole = depth_in // LANES * LANES
-    padded = [cats[layer].shape[1] for layer in range(6)]
+    padded = [cats[layer].shape[1] for layer in range(6)] + [cats[5].shape[0]]
 
     def x_copy(c):
         part = pl.ds(c * CHUNK, CHUNK)
         return pltpu.make_async_copy(x_hbm.at[:, part], x_in.at[:, part], x_sems.at[c])
+
+    def first_copy(n):
+        part = pl.ds(n * FIRST, FIRST)
+        return pltpu.make_async_copy(
+            weights_hbm[0].at[:, part], weights_in[0].at[:, part], first_sems.at[n]
+        )
 
     def w_copy(layer):
         target = weights_in[layer]
@@ -123,38 +131,40 @@
             put_rows(0, k, cols, x_in[k : k + LANES, cols], TOP / INPUT_MAX)
         put_rows(0, whole, cols, x_tail[:, cols], TOP / INPUT_MAX)
 
-    def product(layer, c):
+    def product(layer, c, lines):
         depth = padded[layer]
         cols = slice(c * CHUNK, (c + 1) * CHUNK)
         main = jnp.dot(
-            cats[layer][...],
+            cats[layer][lines, :],
             holds[layer % 2][0:depth, cols],
             preferred_element_type=F32,
         )
         rest = jnp.dot(
-            cats8[layer][...],
+            cats8[layer][lines, :],
             holds8[layer % 2][0 : 2 * depth, cols],
             preferred_element_type=F32,
         )
         return main, rest
 
-    def finish(layer, c, main, rest):
+    def finish(layer, c, lines, main, rest):
         cols = slice(c * CHUNK, (c + 1) * CHUNK)
         unit = 1.0 / (WEIGHT_STEP * LOW_STEP * (2.0 if layer < 5 else 1.0))
         if layer == 0:
             shrink, peak = jnp.full((1, CHUNK), INPUT_MAX / TOP, F32), INPUT_MAX
         else:
             shrink, peak = shrinks[layer : layer + 1, cols], peaks[layer : layer + 1, cols]
-        bias = columns[layer][...]
+        bias = columns[layer][lines, :]
         value = main + rest * (shrink * unit)
         value = value + jnp.concatenate([bias] * (CHUNK // LANES), axis=1)
         if layer < 5:
             value = value + value * jnp.tanh(value)
             limit = (sizes[layer] * WEIGHT_MAX[layer]) * peak + BIAS_MAX
             limit = jnp.broadcast_to(jnp.asarray(limit, F32), (1, CHUNK))
-            put_rows(layer + 1, 0, cols, value, TOP / limit)
+            put_rows(layer + 1, lines.start, cols, value, TOP / limit)
             shrinks[layer + 1 : layer + 2, cols] = limit / TOP
             highest = jnp.max(value, axis=0, keepdims=True)
+            if lines.start:
+                highest = jnp.maximum(highest, peaks[layer + 1 : layer + 2, cols])
             peaks[layer + 1 : layer + 2, cols] = jnp.maximum(highest, SILU_DIP)
             return
         for part in range(CHUNK // LANES):
@@ -169,22 +179,30 @@
             )
         out_copy(c).start()
 
-    w_copy(0).start()
-    for c in range(chunks):
-        x_copy(c).start()
-    for i in range(10):
-        small_copy(i).start()
-    w_copy(1).start()
+    def prepare_first(n):
+        first_copy(n).wait()
+        lines = slice(n * FIRST, (n + 1) * FIRST)
+        w_tail[0 : aligned - whole, lines] = weights_in[0][whole:aligned, lines]
+        w_tail[aligned - whole : depth_in - whole, lines] = weights_in[0][
+            aligned:depth_in, lines
+        ]
+        prepare(0, n, sizes[1] // FIRST)
+
+    first_copy(0).start()
+    x_copy(0).start()
+    for n in range(1, sizes[1] // FIRST):
+        first_copy(n).start()
     w_tail[...] = jnp.zeros(w_tail.shape, F32)
     x_tail[...] = jnp.zeros(x_tail.shape, F32)
     weights_in[5][sizes[6] :, :] = jnp.zeros(
         (weights_in[5].shape[0] - sizes[6], sizes[5]), F32
     )
-    w_copy(0).wait()
-    w_tail[0 : aligned - whole, :] = weights_in[0][whole:aligned, :]
-    w_tail[aligned - whole : depth_in - whole, :] = weights_in[0][aligned:depth_in, :]
-    prepare(0, 0, 1)
-    for layer in range(2, 6):
+    prepare_first(0)
+    for c in range(1, chunks):
+        x_copy(c).start()
+    for i in range(10):
+        small_copy(i).start()
+    for layer in range(1, 6):
         w_copy(layer).start()
     x_copy(0).wait()
     prepare_inputs(0)
@@ -192,28 +210,34 @@
     for layer in range(6):
         if 0 < layer < 5:
             w_copy(layer + 1).wait()
-        for c in range(chunks):
-            main, rest = product(layer, c)
-            if layer == 0 and c == 0:
-                for i in range(10):
-                    small_copy(i).wait()
-                bias_columns(0)
-                for i in range(1, chunks):
-                    x_copy(i).wait()
-                    prepare_inputs(i)
-                w_copy(1).wait()
-            if layer < 5:
-                prepare(layer + 1, c, chunks)
-                if c == chunks - 1:
-                    bias_columns(layer + 1)
-            if layer == 4 and c == 0:
-                for r in range(rows):
-                    field[r, levels : levels + 1, :] = along[r : r + 1, :]
-                    field[r, levels + 1 : levels + 2, :] = across[r : r + 1, :]
-                    field[r, levels + 2 : levels_wide, :] = jnp.zeros(
-                        (levels_wide - levels - 2, LANES), F32
-                    )
-            finish(layer, c, main, rest)
+        span = FIRST if layer == 0 else padded[layer + 1]
+        for n in range(0, padded[layer + 1], span):
+            lines = slice(n, n + span)
+            for c in range(chunks):
+                main, rest = product(layer, c, lines)
+                if layer == 0 and n == 0 and c == 0:
+                    for i in range(10):
+                        small_copy(i).wait()
+                    bias_columns(0)
+                    for i in range(1, chunks):
+                        x_copy(i).wait()
+                        prepare_inputs(i)
+                elif layer == 0 and c == chunks - 1 and n + span < sizes[1]:
+                    prepare_first(n // FIRST + 1)
+                if layer == 0 and n + span == sizes[1] or 0 < layer < 5:
+                    if layer == 0 and c == 0:
+                        w_copy(1).wait()
+                    prepare(layer + 1, c, chunks)
+                    if c == chunks - 1:
+                        bias_columns(layer + 1)
+                if layer == 4 and c == 0:
+                    for r in range(rows):
+                        field[r, levels : levels + 1, :] = along[r : r + 1, :]
+                        field[r, levels + 1 : levels + 2, :] = across[r : r + 1, :]
+                        field[r, levels + 2 : levels_wide, :] = jnp.zeros(
+                            (levels_wide - levels - 2, LANES), F32
+                        )
+                finish(layer, c, lines, main, rest)
 
     odd = lax.rem(lax.axis_index(axis), 2)
     leaving = [
@@ -223,7 +247,7 @@
         pltpu.make_async_copy(
             field.at[pl.ds((rows - HALO) * (1 - odd), HALO)], pay_b, field_sems.at[1]
         ),
-        pltpu.make_async_copy(field, field_hbm, field_sems.at[2]),
+        pltpu.make_async_copy(field, field_hbm.at[pl.ds(0, rows)], field_sems.at[2]),
     ]
     for copy in leaving:
         copy.start()
@@ -249,7 +273,7 @@
         functools.partial(network_kernel, sizes=sizes, levels=levels, axis=axis),
         out_shape=(
             jax.ShapeDtypeStruct((sizes[6], width), F32),
-            jax.ShapeDtypeStruct((rows, levels_wide, LANES), F32),
+            jax.ShapeDtypeStruct((ROOM, levels_wide, LANES), F32),
             jax.ShapeDtypeStruct((HALO, levels_wide, LANES), F32),
             jax.ShapeDtypeStruct((HALO, levels_wide, LANES), F32),
         ),
@@ -281,6 +305,7 @@
             pltpu.SemaphoreType.DMA((chunks,)),
             pltpu.SemaphoreType.DMA((10,)),
             pltpu.SemaphoreType.DMA((3,)),
+            pltpu.SemaphoreType.DMA((sizes[1] // FIRST,)),
         ],
         compiler_params=pltpu.CompilerParams(vmem_limit_bytes=NETWORK_VMEM),
         cost_estimate=pl.CostEstimate(
@@ -301,13 +326,23 @@
     return values[0] if len(values) == 1 else jnp.concatenate(values, axis=0)
 
 
-def advect_kernel(field, got_a, got_b, out, wide, speeds, sem, *, levels, axis):
-    rows = field.shape[0]
+def advect_kernel(
+    field, got_a, got_b, out, wide, speeds, held, in_sems, out_sems, *, levels, axis
+):
+    rows = wide.shape[0] - 2 * HALO
     odd = lax.rem(lax.axis_index(axis), 2)
-    own = pltpu.make_async_copy(field, wide.at[pl.ds(HALO, rows)], sem)
-    own.start()
-    wide[pl.ds((HALO + rows) * odd, HALO)] = got_a[...]
-    wide[pl.ds((HALO + rows) * (1 - odd), HALO)] = got_b[...]
+    arriving = [
+        pltpu.make_async_copy(source, wide.at[pl.ds(start, source.shape[0])], in_sems.at[n])
+        for n, (source, start) in enumerate(
+            [
+                (field.at[pl.ds(0, rows)], HALO),
+                (got_a, (HALO + rows) * odd),
+                (got_b, (HALO + rows) * (1 - odd)),
+            ]
+        )
+    ]
+    for copy in arriving:
+        copy.start()
 
     def place(i):
         for kind in range(2):
@@ -317,19 +352,34 @@
             speeds[2 * kind, i] = jnp.maximum(courant, 0.0)
             speeds[2 * kind + 1, i] = jnp.minimum(courant, 0.0)
 
-    for i in range(HALO):
-        place(i)
-        place(HALO + rows + i)
-    own.wait()
-    for i in range(HALO, HALO + rows):
+    for copy in arriving:
+        copy.wait()
+    for i in range(rows + 2 * HALO):
         place(i)
     groups = wide.shape[1] // GROUP
+    span = GROUP * rows
+
+    def leaving(g, start, size):
+        return pltpu.make_async_copy(
+            held.at[pl.ds(start, size)], out.at[pl.ds(start, size)], out_sems.at[g]
+        )
+
+    last = out.shape[0] - (groups - 1) * span
 
     def group(g, carry):
-        wavefront(g, groups, levels, out, wide, speeds, rows)
+        wavefront(g, groups, levels, held, wide, speeds, rows)
+
+        @pl.when(g < groups - 1)
+        def _():
+            leaving(g, pl.multiple_of(g * span, span), span).start()
+
         return carry
 
     lax.fori_loop(0, groups, group, 0)
+    leaving(groups - 1, (groups - 1) * span, last).start()
+    for g in range(groups - 1):
+        leaving(g, g * span, span).wait()
+    leaving(groups - 1, (groups - 1) * span, last).wait()
 
 
 def wavefront(g, groups, levels, out, wide, speeds, rows):
@@ -411,18 +461,20 @@
                 out[lines, :] = value
 
 
-def advect(field, got_a, got_b, levels, axis):
-    rows, levels_wide, across = field.shape
-    vmem = pl.BlockSpec(memory_space=pltpu.VMEM)
+def advect(field, got_a, got_b, rows, levels, axis):
+    _, levels_wide, across = field.shape
+    hbm = pl.BlockSpec(memory_space=pl.ANY)
     return pl.pallas_call(
         functools.partial(advect_kernel, levels=levels, axis=axis),
         out_shape=jax.ShapeDtypeStruct((levels * rows, across), F32),
-        in_specs=[pl.BlockSpec(memory_space=pl.ANY), vmem, vmem],
-        out_specs=vmem,
+        in_specs=[hbm] * 3,
+        out_specs=hbm,
         scratch_shapes=[
             pltpu.VMEM((rows + 2 * HALO, levels_wide, across), F32),
             pltpu.VMEM((4, rows + 2 * HALO, 8, across), F32),
-            pltpu.SemaphoreType.DMA,
+            pltpu.VMEM((levels * rows, across), F32),
+            pltpu.SemaphoreType.DMA((3,)),
+            pltpu.SemaphoreType.DMA((levels_wide // GROUP,)),
         ],
         compiler_params=pltpu.CompilerParams(vmem_limit_bytes=ADVECT_VMEM),
         name="advect_sections",
@@ -448,7 +500,7 @@
     inner = [(i, i + 1 if i % 2 == 0 else i - 1) for i in range(count)]
     got_a = lax.ppermute(pay_a, "gx", outer)
     got_b = lax.ppermute(pay_b, "gx", inner)
-    advected = advect(field, got_a, got_b, levels, "gx")
+    advected = advect(field, got_a, got_b, rows, levels, "gx")
     return tendencies.T, advected.reshape(levels, rows, across)
 
 

time: 33.3 us -> 35.5 us (1.066)
  Pallas kernels: 22.4 us -> 25.5 us
  local copies, waits for them, and re-layouts: 0.95 us -> 0 us
    pallas_call x1, Pallas kernels: 19.2 us -> 21.4 us  [network(): pl.pallas_call(functools.partial(network_kernel, sizes=sizes, levels=leve...]
    unnamed x2 -> x0, local copies, waits for them, and re-layouts: 0.95 us -> none
    pallas_call x1, Pallas kernels: 3.17 us -> 4.06 us  [advect(): pl.pallas_call(functools.partial(advect_kernel, levels=levels, axis=axis)...]
where the time goes in v1:
time: 35.5 us; the launch traced here: 35.4 us
  Pallas kernels  25.5 us (72%)
  starting transfers between devices  5.49 us (15%)
  waiting for transfers between devices  3.56 us (10%)
  between operations  0.81 us (2%)
    pallas_call x1, Pallas kernels, network(): pl.pallas_call(functools.partial(network_kernel, sizes=sizes, levels=leve...  21.4 us
    ppermute x1, starting transfers between devices, shards(): got_a = lax.ppermute(pay_a, 'gx', outer)  5.48 us
    pallas_call x1, Pallas kernels, advect(): pl.pallas_call(functools.partial(advect_kernel, levels=levels, axis=axis)...  4.06 us
    ppermute x1, waiting for transfers between devices, shards(): got_a = lax.ppermute(pay_a, 'gx', outer)  3.56 us
  transfers between devices with their start and end apart: 2, of which 1 were waited for; matrix products, arithmetic and copies ran while one was open for 0% of the time, Pallas kernels for 0%

profile of v1, /device:TPU:0, one launch (start us, length us, event | category | flops | bytes accessed | tf_op | source)
XLA Modules:
  0.0 35.4 jit_solution(14746891180600647351)
XLA Ops:
  0.6 21.4 %column_network.1 = (f32[368,1024]{1,0:T(8,128)}, f32[128,64,128]{2,1,0:T(8,128)}, f32[6,64,128]{2,1,0:T(8,128)}, f32[6,64,128]{2,1,0:T(8,128)}) custom-call(s32[8,128]{1,0:T(8,128)} %bitcast.10, f32[480,128]{1,0:T(8,128)} %bitcast.9, f32[8,128]{1,0:T(8,128)} %refs_2_.1, f32[8,128]{1,0:T(8,128)} %refs_3_.1, f32[768]{0:T(1024)} %refs_4_.1, f32[640]{0:T(1024)} %refs_5_.1, ...), custom_call_target="tpu_custom_call" | custom-call | flops 9092202496 | bytes 14000000 | tf_op jit(solution)/shard_map/column_network/pallas_call | solution.py:272
  22.1 5.5 %collective-permute-start = (f32[6,64,128]{2,1,0:T(8,128)}, f32[6,64,128]{2,1,0:T(8,128)S(1)}, u32[]{:S(2)}, u32[]{:S(2)}) collective-permute-start(f32[6,64,128]{2,1,0:T(8,128)} %get-tuple-element.8), channel_id=1, source_target_pairs={{0,15},{1,2},{2,1},{3,4},{4,3},{5,6},{6,5},{7,8},{8,7},{9,10},{10,... | collective-permute-start | bytes 589832 | tf_op jit(solution)/shard_map/ppermute | solution.py:501
  27.6 0.0 collective-permute-start.1
  27.6 3.6 %collective-permute-done.got_a = f32[6,64,128]{2,1,0:T(8,128)S(1)} collective-permute-done((f32[6,64,128]{2,1,0:T(8,128)}, f32[6,64,128]{2,1,0:T(8,128)S(1)}, u32[]{:S(2)}, u32[]{:S(2)}) %collective-permute-start) | collective-permute-done | bytes 196640 | tf_op jit(solution)/shard_map/ppermute | solution.py:501
  31.1 0.0 collective-permute-done.1.got_b
  31.1 4.1 %advect_sections.1 = f32[480,128]{1,0:T(8,128)} custom-call(f32[128,64,128]{2,1,0:T(8,128)} %get-tuple-element.7.field, f32[6,64,128]{2,1,0:T(8,128)S(1)} %collective-permute-done.got_a, f32[6,64,128]{2,1,0:T(8,128)S(1)} %collective-permute-done.1.got_b), custom_call_target="tpu_custom_call" | custom-call | tf_op jit(solution)/shard_map/advect_sections/pallas_call | solution.py:467
Async XLA Ops:
  22.1 9.1 %collective-permute-start = (f32[6,64,128]{2,1,0:T(8,128)}, f32[6,64,128]{2,1,0:T(8,128)S(1)}, u32[]{:S(2)}, u32[]{:S(2)}) collective-permute-start(f32[6,64,128]{2,1,0:T(8,128)} %get-tuple-element.8), channel_id=1, source_target_pairs={{0,15},{1,2},{2,1},{3,4},{4,3},{5,6},{6,5},{7,8},{8,7},{9,10},{10,... | collective-permute-start | bytes 589832 | tf_op jit(solution)/shard_map/ppermute | solution.py:501
  27.6 3.6 %collective-permute-start.1 = (f32[6,64,128]{2,1,0:T(8,128)}, f32[6,64,128]{2,1,0:T(8,128)S(1)}, u32[]{:S(2)}, u32[]{:S(2)}) collective-permute-start(f32[6,64,128]{2,1,0:T(8,128)} %get-tuple-element.9), channel_id=1, source_target_pairs={{0,1},{1,0},{2,3},{3,2},{4,5},{5,4},{6,7},{7,6},{8,9},{9,8},{10,11... | collective-permute-start | bytes 589832 | tf_op jit(solution)/shard_map/ppermute | solution.py:502

commit v2 on v0

--- a/solution.py
+++ b/solution.py
@@ -19,7 +19,8 @@
 WEIGHT_STEP = 2.0**10
 LOW_STEP = 2.0**8
 NETWORK_VMEM = 60_000_000
-ADVECT_VMEM = 8 * 2**20
+ADVECT_VMEM = 54_000_000
+ROOM = 128
 
 
 def round_up(value, unit):
@@ -123,20 +124,21 @@
             put_rows(0, k, cols, x_in[k : k + LANES, cols], TOP / INPUT_MAX)
         put_rows(0, whole, cols, x_tail[:, cols], TOP / INPUT_MAX)
 
-    def product(layer, c):
-        depth = padded[layer]
+    def main_product(layer, c):
         cols = slice(c * CHUNK, (c + 1) * CHUNK)
-        main = jnp.dot(
+        return jnp.dot(
             cats[layer][...],
-            holds[layer % 2][0:depth, cols],
+            holds[layer % 2][0 : padded[layer], cols],
             preferred_element_type=F32,
         )
-        rest = jnp.dot(
+
+    def rest_product(layer, c):
+        cols = slice(c * CHUNK, (c + 1) * CHUNK)
+        return jnp.dot(
             cats8[layer][...],
-            holds8[layer % 2][0 : 2 * depth, cols],
+            holds8[layer % 2][0 : 2 * padded[layer], cols],
             preferred_element_type=F32,
         )
-        return main, rest
 
     def finish(layer, c, main, rest):
         cols = slice(c * CHUNK, (c + 1) * CHUNK)
@@ -193,7 +195,7 @@
         if 0 < layer < 5:
             w_copy(layer + 1).wait()
         for c in range(chunks):
-            main, rest = product(layer, c)
+            main = main_product(layer, c)
             if layer == 0 and c == 0:
                 for i in range(10):
                     small_copy(i).wait()
@@ -204,8 +206,7 @@
                 w_copy(1).wait()
             if layer < 5:
                 prepare(layer + 1, c, chunks)
-                if c == chunks - 1:
-                    bias_columns(layer + 1)
+            rest = rest_product(layer, c)
             if layer == 4 and c == 0:
                 for r in range(rows):
                     field[r, levels : levels + 1, :] = along[r : r + 1, :]
@@ -213,6 +214,8 @@
                     field[r, levels + 2 : levels_wide, :] = jnp.zeros(
                         (levels_wide - levels - 2, LANES), F32
                     )
+            if layer < 5 and c == chunks - 1:
+                bias_columns(layer + 1)
             finish(layer, c, main, rest)
 
     odd = lax.rem(lax.axis_index(axis), 2)
@@ -223,7 +226,7 @@
         pltpu.make_async_copy(
             field.at[pl.ds((rows - HALO) * (1 - odd), HALO)], pay_b, field_sems.at[1]
         ),
-        pltpu.make_async_copy(field, field_hbm, field_sems.at[2]),
+        pltpu.make_async_copy(field, field_hbm.at[pl.ds(0, rows)], field_sems.at[2]),
     ]
     for copy in leaving:
         copy.start()
@@ -249,7 +252,7 @@
         functools.partial(network_kernel, sizes=sizes, levels=levels, axis=axis),
         out_shape=(
             jax.ShapeDtypeStruct((sizes[6], width), F32),
-            jax.ShapeDtypeStruct((rows, levels_wide, LANES), F32),
+            jax.ShapeDtypeStruct((ROOM, levels_wide, LANES), F32),
             jax.ShapeDtypeStruct((HALO, levels_wide, LANES), F32),
             jax.ShapeDtypeStruct((HALO, levels_wide, LANES), F32),
         ),
@@ -301,13 +304,23 @@
     return values[0] if len(values) == 1 else jnp.concatenate(values, axis=0)
 
 
-def advect_kernel(field, got_a, got_b, out, wide, speeds, sem, *, levels, axis):
-    rows = field.shape[0]
+def advect_kernel(
+    field, got_a, got_b, out, wide, speeds, held, in_sems, out_sems, *, levels, axis
+):
+    rows = wide.shape[0] - 2 * HALO
     odd = lax.rem(lax.axis_index(axis), 2)
-    own = pltpu.make_async_copy(field, wide.at[pl.ds(HALO, rows)], sem)
-    own.start()
-    wide[pl.ds((HALO + rows) * odd, HALO)] = got_a[...]
-    wide[pl.ds((HALO + rows) * (1 - odd), HALO)] = got_b[...]
+    arriving = [
+        pltpu.make_async_copy(source, wide.at[pl.ds(start, source.shape[0])], in_sems.at[n])
+        for n, (source, start) in enumerate(
+            [
+                (field, HALO),
+                (got_a, (HALO + rows) * odd),
+                (got_b, (HALO + rows) * (1 - odd)),
+            ]
+        )
+    ]
+    for copy in arriving:
+        copy.start()
 
     def place(i):
         for kind in range(2):
@@ -317,19 +330,34 @@
             speeds[2 * kind, i] = jnp.maximum(courant, 0.0)
             speeds[2 * kind + 1, i] = jnp.minimum(courant, 0.0)
 
-    for i in range(HALO):
-        place(i)
-        place(HALO + rows + i)
-    own.wait()
-    for i in range(HALO, HALO + rows):
+    for copy in arriving:
+        copy.wait()
+    for i in range(rows + 2 * HALO):
         place(i)
     groups = wide.shape[1] // GROUP
+    span = GROUP * rows
+
+    def leaving(g, start, size):
+        return pltpu.make_async_copy(
+            held.at[pl.ds(start, size)], out.at[pl.ds(start, size)], out_sems.at[g]
+        )
+
+    last = out.shape[0] - (groups - 1) * span
 
     def group(g, carry):
-        wavefront(g, groups, levels, out, wide, speeds, rows)
+        wavefront(g, groups, levels, held, wide, speeds, rows)
+
+        @pl.when(g < groups - 1)
+        def _():
+            leaving(g, pl.multiple_of(g * span, span), span).start()
+
         return carry
 
     lax.fori_loop(0, groups, group, 0)
+    leaving(groups - 1, (groups - 1) * span, last).start()
+    for g in range(groups - 1):
+        leaving(g, g * span, span).wait()
+    leaving(groups - 1, (groups - 1) * span, last).wait()
 
 
 def wavefront(g, groups, levels, out, wide, speeds, rows):
@@ -411,18 +439,41 @@
                 out[lines, :] = value
 
 
+def stage_kernel(field, own, sem):
+    copy = pltpu.make_async_copy(field.at[pl.ds(0, own.shape[0])], own, sem)
+    copy.start()
+    copy.wait()
+
+
+def stage(field, rows):
+    return pl.pallas_call(
+        stage_kernel,
+        out_shape=jax.ShapeDtypeStruct((rows, *field.shape[1:]), F32),
+        in_specs=[pl.BlockSpec(memory_space=pl.ANY)],
+        out_specs=pl.BlockSpec(memory_space=pltpu.VMEM),
+        scratch_shapes=[pltpu.SemaphoreType.DMA],
+        compiler_params=pltpu.CompilerParams(vmem_limit_bytes=ADVECT_VMEM),
+        cost_estimate=pl.CostEstimate(
+            flops=0, bytes_accessed=4_000_000, transcendentals=0
+        ),
+        name="stage_rows",
+    )(field)
+
+
 def advect(field, got_a, got_b, levels, axis):
     rows, levels_wide, across = field.shape
-    vmem = pl.BlockSpec(memory_space=pltpu.VMEM)
+    hbm = pl.BlockSpec(memory_space=pl.ANY)
     return pl.pallas_call(
         functools.partial(advect_kernel, levels=levels, axis=axis),
         out_shape=jax.ShapeDtypeStruct((levels * rows, across), F32),
-        in_specs=[pl.BlockSpec(memory_space=pl.ANY), vmem, vmem],
-        out_specs=vmem,
+        in_specs=[hbm] * 3,
+        out_specs=hbm,
         scratch_shapes=[
             pltpu.VMEM((rows + 2 * HALO, levels_wide, across), F32),
             pltpu.VMEM((4, rows + 2 * HALO, 8, across), F32),
-            pltpu.SemaphoreType.DMA,
+            pltpu.VMEM((levels * rows, across), F32),
+            pltpu.SemaphoreType.DMA((3,)),
+            pltpu.SemaphoreType.DMA((levels_wide // GROUP,)),
         ],
         compiler_params=pltpu.CompilerParams(vmem_limit_bytes=ADVECT_VMEM),
         name="advect_sections",
@@ -448,7 +499,7 @@
     inner = [(i, i + 1 if i % 2 == 0 else i - 1) for i in range(count)]
     got_a = lax.ppermute(pay_a, "gx", outer)
     got_b = lax.ppermute(pay_b, "gx", inner)
-    advected = advect(field, got_a, got_b, levels, "gx")
+    advected = advect(stage(field, rows), got_a, got_b, levels, "gx")
     return tendencies.T, advected.reshape(levels, rows, across)
 
 

time: 33.3 us -> 33.1 us (level)
  Pallas kernels: 22.4 us -> 24 us
  waiting for transfers between devices: 3.56 us -> 2.6 us
  local copies, waits for them, and re-layouts: 0.95 us -> 0 us
    ppermute x1, waiting for transfers between devices: 3.56 us -> 2.6 us  [shards(): got_a = lax.ppermute(pay_a, 'gx', outer)]
    pallas_call x0 -> x1, Pallas kernels: none -> 0.96 us  [stage(): pl.pallas_call(stage_kernel, out_shape=jax.ShapeDtypeStruct((rows, *field...]
    unnamed x2 -> x0, local copies, waits for them, and re-layouts: 0.95 us -> none
    pallas_call x1, Pallas kernels: 3.17 us -> 3.64 us  [advect(): pl.pallas_call(functools.partial(advect_kernel, levels=levels, axis=axis)...]
  transfers between devices with their start and end apart: 2 -> 2, of which waited for: 1 -> 1; matrix products, arithmetic and copies ran while one was open for 0% -> 0% of each run, Pallas kernels for 0% -> 3%
where the time goes in v2:
time: 33.1 us; the launch traced here: 32.9 us
  Pallas kernels  24 us (73%)
  starting transfers between devices  5.49 us (17%)
  waiting for transfers between devices  2.6 us (8%)
  between operations  0.82 us (2%)
    pallas_call x1, Pallas kernels, network(): pl.pallas_call(functools.partial(network_kernel, sizes=sizes, levels=leve...  19.4 us
    ppermute x1, starting transfers between devices, shards(): got_a = lax.ppermute(pay_a, 'gx', outer)  5.48 us
    pallas_call x1, Pallas kernels, advect(): pl.pallas_call(functools.partial(advect_kernel, levels=levels, axis=axis)...  3.64 us
    ppermute x1, waiting for transfers between devices, shards(): got_a = lax.ppermute(pay_a, 'gx', outer)  2.6 us
    pallas_call x1, Pallas kernels, stage(): pl.pallas_call(stage_kernel, out_shape=jax.ShapeDtypeStruct((rows, *field...  0.96 us
  transfers between devices with their start and end apart: 2, of which 1 were waited for; matrix products, arithmetic and copies ran while one was open for 0% of the time, Pallas kernels for 3%

profile of v2, /device:TPU:0, one launch (start us, length us, event | category | flops | bytes accessed | tf_op | source)
XLA Modules:
  0.0 32.9 jit_solution(10683782610227505547)
XLA Ops:
  0.6 19.4 %column_network.1 = (f32[368,1024]{1,0:T(8,128)}, f32[128,64,128]{2,1,0:T(8,128)}, f32[6,64,128]{2,1,0:T(8,128)}, f32[6,64,128]{2,1,0:T(8,128)}) custom-call(s32[8,128]{1,0:T(8,128)} %bitcast.10, f32[480,128]{1,0:T(8,128)} %bitcast.9, f32[8,128]{1,0:T(8,128)} %refs_2_.1, f32[8,128]{1,0:T(8,128)} %refs_3_.1, f32[768]{0:T(1024)} %refs_4_.1, f32[640]{0:T(1024)} %refs_5_.1, ...), custom_call_target="tpu_custom_call" | custom-call | flops 9092202496 | bytes 14000000 | tf_op jit(solution)/shard_map/column_network/pallas_call | solution.py:251
  20.0 5.5 %collective-permute-start = (f32[6,64,128]{2,1,0:T(8,128)}, f32[6,64,128]{2,1,0:T(8,128)S(1)}, u32[]{:S(2)}, u32[]{:S(2)}) collective-permute-start(f32[6,64,128]{2,1,0:T(8,128)} %get-tuple-element.8), channel_id=1, source_target_pairs={{0,15},{1,2},{2,1},{3,4},{4,3},{5,6},{6,5},{7,8},{8,7},{9,10},{10,... | collective-permute-start | bytes 589832 | tf_op jit(solution)/shard_map/ppermute | solution.py:500
  25.5 0.0 collective-permute-start.1
  25.5 1.0 %stage_rows.1.field = f32[8,64,128]{2,1,0:T(8,128)S(1)} custom-call(f32[128,64,128]{2,1,0:T(8,128)} %get-tuple-element.7.field), custom_call_target="tpu_custom_call" | custom-call | bytes 4000000 | tf_op jit(solution)/shard_map/stage_rows/pallas_call | solution.py:449
  26.5 2.6 %collective-permute-done.got_a = f32[6,64,128]{2,1,0:T(8,128)S(1)} collective-permute-done((f32[6,64,128]{2,1,0:T(8,128)}, f32[6,64,128]{2,1,0:T(8,128)S(1)}, u32[]{:S(2)}, u32[]{:S(2)}) %collective-permute-start) | collective-permute-done | bytes 196640 | tf_op jit(solution)/shard_map/ppermute | solution.py:500
  29.1 0.0 collective-permute-done.1.got_b
  29.1 3.6 %advect_sections.1 = f32[480,128]{1,0:T(8,128)} custom-call(f32[8,64,128]{2,1,0:T(8,128)S(1)} %stage_rows.1.field, f32[6,64,128]{2,1,0:T(8,128)S(1)} %collective-permute-done.got_a, f32[6,64,128]{2,1,0:T(8,128)S(1)} %collective-permute-done.1.got_b), custom_call_target="tpu_custom_call" | custom-call | tf_op jit(solution)/shard_map/advect_sections/pallas_call | solution.py:466
Async XLA Ops:
  20.0 9.1 %collective-permute-start = (f32[6,64,128]{2,1,0:T(8,128)}, f32[6,64,128]{2,1,0:T(8,128)S(1)}, u32[]{:S(2)}, u32[]{:S(2)}) collective-permute-start(f32[6,64,128]{2,1,0:T(8,128)} %get-tuple-element.8), channel_id=1, source_target_pairs={{0,15},{1,2},{2,1},{3,4},{4,3},{5,6},{6,5},{7,8},{8,7},{9,10},{10,... | collective-permute-start | bytes 589832 | tf_op jit(solution)/shard_map/ppermute | solution.py:500
  25.5 3.6 %collective-permute-start.1 = (f32[6,64,128]{2,1,0:T(8,128)}, f32[6,64,128]{2,1,0:T(8,128)S(1)}, u32[]{:S(2)}, u32[]{:S(2)}) collective-permute-start(f32[6,64,128]{2,1,0:T(8,128)} %get-tuple-element.9), channel_id=1, source_target_pairs={{0,1},{1,0},{2,3},{3,2},{4,5},{5,4},{6,7},{7,6},{8,9},{9,8},{10,11... | collective-permute-start | bytes 589832 | tf_op jit(solution)/shard_map/ppermute | solution.py:501

commit v3 on v2

--- a/solution.py
+++ b/solution.py
@@ -16,6 +16,8 @@
 INPUT_MAX = 6.0
 SILU_DIP = 0.28
 TOP = 440.0
+INPUT_SCALE = 72.0
+MIXED = (0, 1, 3, 4)
 WEIGHT_STEP = 2.0**10
 LOW_STEP = 2.0**8
 NETWORK_VMEM = 60_000_000
@@ -42,7 +44,7 @@
     depth_in = sizes[0]
     aligned = depth_in // 8 * 8
     whole = depth_in // LANES * LANES
-    padded = [cats[layer].shape[1] for layer in range(6)]
+    padded = [round_up(sizes[layer], LANES) for layer in range(6)]
 
     def x_copy(c):
         part = pl.ds(c * CHUNK, CHUNK)
@@ -84,10 +86,14 @@
             block = block * 0.5
         high = block.astype(BF16)
         low = block - high.astype(F32)
+        cats[layer][lines, k : k + LANES] = high
+        if layer not in MIXED:
+            cats[layer][lines, depth + k : depth + k + LANES] = high
+            cats[layer][lines, 2 * depth + k : 2 * depth + k + LANES] = low.astype(BF16)
+            return
         step = WEIGHT_STEP * (2.0 if layer < 5 else 1.0)
         lanes, far = slice(k, k + LANES), slice(depth + k, depth + k + LANES)
-        cats[layer][lines, lanes] = high
-        cats8[layer][lines, lanes] = (block * step).astype(F8)
+        cats8[layer][lines, lanes] = (high * BF16(step)).astype(F8)
         cats8[layer][lines, far] = (low * (step * LOW_STEP)).astype(F8)
 
     def prepare(layer, part, parts):
@@ -111,28 +117,38 @@
         high = value.astype(BF16)
         low = value - high.astype(F32)
         size = value.shape[0]
-        holds[layer % 2][start : start + size, cols] = high
-        hold8 = holds8[layer % 2]
-        hold8[start : start + size, cols] = (low * (scale * LOW_STEP)).astype(F8)
-        hold8[depth + start : depth + start + size, cols] = (value * scale).astype(F8)
+        hold, hold8 = holds[layer % 2], holds8[layer % 2]
+        near = slice(start, start + size)
+        middle = slice(depth + start, depth + start + size)
+        hold[near, cols] = high
+        if layer not in MIXED:
+            hold[middle, cols] = low.astype(BF16)
+            hold[2 * depth + start : 2 * depth + start + size, cols] = high
+            return
+        hold8[near, cols] = (low * (scale * LOW_STEP)).astype(F8)
+        hold8[middle, cols] = (high * scale.astype(BF16)).astype(F8)
+
+    first_scale = jnp.full((1, CHUNK), INPUT_SCALE, F32)
 
     def prepare_inputs(c):
         cols = slice(c * CHUNK, (c + 1) * CHUNK)
         x_tail[0 : aligned - whole, cols] = x_in[whole:aligned, cols]
         x_tail[aligned - whole : depth_in - whole, cols] = x_in[aligned:depth_in, cols]
         for k in range(0, whole, LANES):
-            put_rows(0, k, cols, x_in[k : k + LANES, cols], TOP / INPUT_MAX)
-        put_rows(0, whole, cols, x_tail[:, cols], TOP / INPUT_MAX)
+            put_rows(0, k, cols, x_in[k : k + LANES, cols], first_scale)
+        put_rows(0, whole, cols, x_tail[:, cols], first_scale)
 
     def main_product(layer, c):
         cols = slice(c * CHUNK, (c + 1) * CHUNK)
         return jnp.dot(
             cats[layer][...],
-            holds[layer % 2][0 : padded[layer], cols],
+            holds[layer % 2][0 : cats[layer].shape[1], cols],
             preferred_element_type=F32,
         )
 
     def rest_product(layer, c):
+        if layer not in MIXED:
+            return None
         cols = slice(c * CHUNK, (c + 1) * CHUNK)
         return jnp.dot(
             cats8[layer][...],
@@ -143,21 +159,24 @@
     def finish(layer, c, main, rest):
         cols = slice(c * CHUNK, (c + 1) * CHUNK)
         unit = 1.0 / (WEIGHT_STEP * LOW_STEP * (2.0 if layer < 5 else 1.0))
-        if layer == 0:
-            shrink, peak = jnp.full((1, CHUNK), INPUT_MAX / TOP, F32), INPUT_MAX
-        else:
-            shrink, peak = shrinks[layer : layer + 1, cols], peaks[layer : layer + 1, cols]
+        value = main
+        if layer in MIXED:
+            shrink = shrinks[layer : layer + 1, cols] if layer else 1.0 / first_scale
+            value = value + rest * (shrink * unit)
+        peak = peaks[layer : layer + 1, cols] if layer else INPUT_MAX
         bias = columns[layer][...]
-        value = main + rest * (shrink * unit)
         value = value + jnp.concatenate([bias] * (CHUNK // LANES), axis=1)
         if layer < 5:
             value = value + value * jnp.tanh(value)
             limit = (sizes[layer] * WEIGHT_MAX[layer]) * peak + BIAS_MAX
             limit = jnp.broadcast_to(jnp.asarray(limit, F32), (1, CHUNK))
-            put_rows(layer + 1, 0, cols, value, TOP / limit)
-            shrinks[layer + 1 : layer + 2, cols] = limit / TOP
-            highest = jnp.max(value, axis=0, keepdims=True)
-            peaks[layer + 1 : layer + 2, cols] = jnp.maximum(highest, SILU_DIP)
+            scale = (TOP / limit).astype(BF16).astype(F32)
+            put_rows(layer + 1, 0, cols, value, scale)
+            if layer + 1 in MIXED:
+                shrinks[layer + 1 : layer + 2, cols] = 1.0 / scale
+            if layer + 2 in MIXED:
+                highest = jnp.max(value, axis=0, keepdims=True)
+                peaks[layer + 1 : layer + 2, cols] = jnp.maximum(highest, SILU_DIP)
             return
         for part in range(CHUNK // LANES):
             r = c * (CHUNK // LANES) + part
@@ -262,7 +281,10 @@
             pltpu.VMEM(x.shape, F32),
             *[pltpu.VMEM(w.shape, F32) for w in weights[:5]],
             pltpu.VMEM((padded[6], sizes[5]), F32),
-            *[pltpu.VMEM((padded[i + 1], padded[i]), BF16) for i in range(6)],
+            *[
+                pltpu.VMEM((padded[i + 1], padded[i] * (1 if i in MIXED else 3)), BF16)
+                for i in range(6)
+            ],
             *[pltpu.VMEM((padded[i + 1], 2 * padded[i]), F8) for i in range(6)],
             *[pltpu.VMEM((padded[i + 1], LANES), F32) for i in range(6)],
             pltpu.VMEM(inverse.shape, jnp.int32),
@@ -270,7 +292,7 @@
             pltpu.VMEM(along.shape, F32),
             pltpu.VMEM(across.shape, F32),
             *[pltpu.VMEM(b.shape, F32) for b in biases],
-            *[pltpu.VMEM((deepest, width), BF16)] * 2,
+            *[pltpu.VMEM((3 * deepest, width), BF16)] * 2,
             *[pltpu.VMEM((2 * deepest, width), F8)] * 2,
             pltpu.VMEM((tail, sizes[1]), F32),
             pltpu.VMEM((tail, width), F32),
@@ -305,22 +327,13 @@
 
 
 def advect_kernel(
-    field, got_a, got_b, out, wide, speeds, held, in_sems, out_sems, *, levels, axis
+    field, got_a, got_b, out, wide, speeds, held, out_sems, *, levels, axis
 ):
-    rows = wide.shape[0] - 2 * HALO
+    rows = field.shape[0]
     odd = lax.rem(lax.axis_index(axis), 2)
-    arriving = [
-        pltpu.make_async_copy(source, wide.at[pl.ds(start, source.shape[0])], in_sems.at[n])
-        for n, (source, start) in enumerate(
-            [
-                (field, HALO),
-                (got_a, (HALO + rows) * odd),
-                (got_b, (HALO + rows) * (1 - odd)),
-            ]
-        )
-    ]
-    for copy in arriving:
-        copy.start()
+    wide[HALO : HALO + rows] = field[...]
+    wide[pl.ds((HALO + rows) * odd, HALO)] = got_a[...]
+    wide[pl.ds((HALO + rows) * (1 - odd), HALO)] = got_b[...]
 
     def place(i):
         for kind in range(2):
@@ -330,8 +343,6 @@
             speeds[2 * kind, i] = jnp.maximum(courant, 0.0)
             speeds[2 * kind + 1, i] = jnp.minimum(courant, 0.0)
 
-    for copy in arriving:
-        copy.wait()
     for i in range(rows + 2 * HALO):
         place(i)
     groups = wide.shape[1] // GROUP
@@ -462,17 +473,16 @@
 
 def advect(field, got_a, got_b, levels, axis):
     rows, levels_wide, across = field.shape
-    hbm = pl.BlockSpec(memory_space=pl.ANY)
+    vmem, hbm = pl.BlockSpec(memory_space=pltpu.VMEM), pl.BlockSpec(memory_space=pl.ANY)
     return pl.pallas_call(
         functools.partial(advect_kernel, levels=levels, axis=axis),
         out_shape=jax.ShapeDtypeStruct((levels * rows, across), F32),
-        in_specs=[hbm] * 3,
+        in_specs=[vmem] * 3,
         out_specs=hbm,
         scratch_shapes=[
             pltpu.VMEM((rows + 2 * HALO, levels_wide, across), F32),
             pltpu.VMEM((4, rows + 2 * HALO, 8, across), F32),
             pltpu.VMEM((levels * rows, across), F32),
-            pltpu.SemaphoreType.DMA((3,)),
             pltpu.SemaphoreType.DMA((levels_wide // GROUP,)),
         ],
         compiler_params=pltpu.CompilerParams(vmem_limit_bytes=ADVECT_VMEM),

time: 33.1 us -> 32.8 us (level)
    pallas_call x1, Pallas kernels: 3.64 us -> 3.13 us  [advect(): pl.pallas_call(functools.partial(advect_kernel, levels=levels, axis=axis)...]
where the time goes in v3:
time: 32.8 us; the launch traced here: 32.6 us
  Pallas kernels  23.7 us (72%)
  starting transfers between devices  5.48 us (17%)
  waiting for transfers between devices  2.6 us (8%)
  between operations  0.82 us (2%)
    pallas_call x1, Pallas kernels, network(): pl.pallas_call(functools.partial(network_kernel, sizes=sizes, levels=leve...  19.6 us
    ppermute x1, starting transfers between devices, shards(): got_a = lax.ppermute(pay_a, 'gx', outer)  5.48 us
    pallas_call x1, Pallas kernels, advect(): pl.pallas_call(functools.partial(advect_kernel, levels=levels, axis=axis)...  3.13 us
    ppermute x1, waiting for transfers between devices, shards(): got_a = lax.ppermute(pay_a, 'gx', outer)  2.6 us
    pallas_call x1, Pallas kernels, stage(): pl.pallas_call(stage_kernel, out_shape=jax.ShapeDtypeStruct((rows, *field...  0.96 us
  transfers between devices with their start and end apart: 2, of which 1 were waited for; matrix products, arithmetic and copies ran while one was open for 0% of the time, Pallas kernels for 3%

profile of v3, /device:TPU:0, one launch (start us, length us, event | category | flops | bytes accessed | tf_op | source)
XLA Modules:
  0.0 32.6 jit_solution(10603528491415556246)
XLA Ops:
  0.6 19.6 %column_network.1 = (f32[368,1024]{1,0:T(8,128)}, f32[128,64,128]{2,1,0:T(8,128)}, f32[6,64,128]{2,1,0:T(8,128)}, f32[6,64,128]{2,1,0:T(8,128)}) custom-call(s32[8,128]{1,0:T(8,128)} %bitcast.10, f32[480,128]{1,0:T(8,128)} %bitcast.9, f32[8,128]{1,0:T(8,128)} %refs_2_.1, f32[8,128]{1,0:T(8,128)} %refs_3_.1, f32[768]{0:T(1024)} %refs_4_.1, f32[640]{0:T(1024)} %refs_5_.1, ...), custom_call_target="tpu_custom_call" | custom-call | flops 9092202496 | bytes 14000000 | tf_op jit(solution)/shard_map/column_network/pallas_call | solution.py:270
  20.3 5.5 %collective-permute-start = (f32[6,64,128]{2,1,0:T(8,128)}, f32[6,64,128]{2,1,0:T(8,128)S(1)}, u32[]{:S(2)}, u32[]{:S(2)}) collective-permute-start(f32[6,64,128]{2,1,0:T(8,128)} %get-tuple-element.8), channel_id=1, source_target_pairs={{0,15},{1,2},{2,1},{3,4},{4,3},{5,6},{6,5},{7,8},{8,7},{9,10},{10,... | collective-permute-start | bytes 589832 | tf_op jit(solution)/shard_map/ppermute | solution.py:510
  25.8 0.0 collective-permute-start.1
  25.8 1.0 %stage_rows.1.field = f32[8,64,128]{2,1,0:T(8,128)S(1)} custom-call(f32[128,64,128]{2,1,0:T(8,128)} %get-tuple-element.7.field), custom_call_target="tpu_custom_call" | custom-call | bytes 4000000 | tf_op jit(solution)/shard_map/stage_rows/pallas_call | solution.py:460
  26.7 2.6 %collective-permute-done.got_a = f32[6,64,128]{2,1,0:T(8,128)S(1)} collective-permute-done((f32[6,64,128]{2,1,0:T(8,128)}, f32[6,64,128]{2,1,0:T(8,128)S(1)}, u32[]{:S(2)}, u32[]{:S(2)}) %collective-permute-start) | collective-permute-done | bytes 196640 | tf_op jit(solution)/shard_map/ppermute | solution.py:510
  29.3 0.0 collective-permute-done.1.got_b
  29.3 3.1 %advect_sections.1 = f32[480,128]{1,0:T(8,128)} custom-call(f32[8,64,128]{2,1,0:T(8,128)S(1)} %stage_rows.1.field, f32[6,64,128]{2,1,0:T(8,128)S(1)} %collective-permute-done.got_a, f32[6,64,128]{2,1,0:T(8,128)S(1)} %collective-permute-done.1.got_b), custom_call_target="tpu_custom_call" | custom-call | tf_op jit(solution)/shard_map/advect_sections/pallas_call | solution.py:477
Async XLA Ops:
  20.3 9.0 %collective-permute-start = (f32[6,64,128]{2,1,0:T(8,128)}, f32[6,64,128]{2,1,0:T(8,128)S(1)}, u32[]{:S(2)}, u32[]{:S(2)}) collective-permute-start(f32[6,64,128]{2,1,0:T(8,128)} %get-tuple-element.8), channel_id=1, source_target_pairs={{0,15},{1,2},{2,1},{3,4},{4,3},{5,6},{6,5},{7,8},{8,7},{9,10},{10,... | collective-permute-start | bytes 589832 | tf_op jit(solution)/shard_map/ppermute | solution.py:510
  25.8 3.6 %collective-permute-start.1 = (f32[6,64,128]{2,1,0:T(8,128)}, f32[6,64,128]{2,1,0:T(8,128)S(1)}, u32[]{:S(2)}, u32[]{:S(2)}) collective-permute-start(f32[6,64,128]{2,1,0:T(8,128)} %get-tuple-element.9), channel_id=1, source_target_pairs={{0,1},{1,0},{2,3},{3,2},{4,5},{5,4},{6,7},{7,6},{8,9},{9,8},{10,11... | collective-permute-start | bytes 589832 | tf_op jit(solution)/shard_map/ppermute | solution.py:511

commit v4 on v3

--- a/solution.py
+++ b/solution.py
@@ -137,6 +137,17 @@
         for k in range(0, whole, LANES):
             put_rows(0, k, cols, x_in[k : k + LANES, cols], first_scale)
         put_rows(0, whole, cols, x_tail[:, cols], first_scale)
+
+    odd = lax.rem(lax.axis_index(axis), 2)
+    leaving = [
+        pltpu.make_async_copy(
+            field.at[pl.ds((rows - HALO) * odd, HALO)], pay_a, field_sems.at[0]
+        ),
+        pltpu.make_async_copy(
+            field.at[pl.ds((rows - HALO) * (1 - odd), HALO)], pay_b, field_sems.at[1]
+        ),
+        pltpu.make_async_copy(field, field_hbm.at[pl.ds(0, rows)], field_sems.at[2]),
+    ]
 
     def main_product(layer, c):
         cols = slice(c * CHUNK, (c + 1) * CHUNK)
@@ -178,16 +189,20 @@
                 highest = jnp.max(value, axis=0, keepdims=True)
                 peaks[layer + 1 : layer + 2, cols] = jnp.maximum(highest, SILU_DIP)
             return
-        for part in range(CHUNK // LANES):
-            r = c * (CHUNK // LANES) + part
-            day = inverse[r : r + 1, :] >= 0
-            shown = jnp.where(
-                day, value[: sizes[6], part * LANES : (part + 1) * LANES], 0.0
-            )
-            tend[:, r * LANES : (r + 1) * LANES] = shown
-            field[r, 0:levels, :] = (
-                tracer[pl.ds(r, levels, stride=rows), :] + shown[0:levels]
-            )
+        for first, stop in ((0, levels_wide), (levels_wide, sizes[6])):
+            for part in range(CHUNK // LANES):
+                r = c * (CHUNK // LANES) + part
+                day = inverse[r : r + 1, :] >= 0
+                lanes = slice(part * LANES, (part + 1) * LANES)
+                shown = jnp.where(day, value[first:stop, lanes], 0.0)
+                tend[first:stop, r * LANES : (r + 1) * LANES] = shown
+                if first == 0:
+                    field[r, 0:levels, :] = (
+                        tracer[pl.ds(r, levels, stride=rows), :] + shown[0:levels]
+                    )
+            if first == 0 and c == chunks - 1:
+                for copy in leaving:
+                    copy.start()
         out_copy(c).start()
 
     w_copy(0).start()
@@ -237,18 +252,6 @@
                 bias_columns(layer + 1)
             finish(layer, c, main, rest)
 
-    odd = lax.rem(lax.axis_index(axis), 2)
-    leaving = [
-        pltpu.make_async_copy(
-            field.at[pl.ds((rows - HALO) * odd, HALO)], pay_a, field_sems.at[0]
-        ),
-        pltpu.make_async_copy(
-            field.at[pl.ds((rows - HALO) * (1 - odd), HALO)], pay_b, field_sems.at[1]
-        ),
-        pltpu.make_async_copy(field, field_hbm.at[pl.ds(0, rows)], field_sems.at[2]),
-    ]
-    for copy in leaving:
-        copy.start()
     for copy in leaving:
         copy.wait()
     for c in range(chunks):
@@ -315,11 +318,9 @@
     )(inverse, tracer, along, across, *biases, x, *weights)
 
 
-def half_minmod(first, second):
-    return 0.5 * (
-        jnp.maximum(jnp.minimum(first, second), 0.0)
-        + jnp.minimum(jnp.maximum(first, second), 0.0)
-    )
+def minmod(first, second):
+    high, low = jnp.maximum(second, 0.0), jnp.minimum(second, 0.0)
+    return jnp.maximum(jnp.minimum(first, high), low)
 
 
 def cat(values):
@@ -375,7 +376,7 @@
     base = pl.multiple_of(g * GROUP, GROUP)
     blocks = GROUP // 8
     keep = levels - (groups - 1) * GROUP
-    fields = [{}, {}, {}]
+    fields, halves = [{}, {}, {}], [{}, {}, {}]
     steps, slopes, fluxes = [{}, {}, {}], [{}, {}, {}], [{}, {}, {}]
     reach = [(-4, rows + 3), (-2, rows + 1), (0, rows - 1)]
     shape = (blocks, 8, LANES)
@@ -396,30 +397,33 @@
         return ahead * lower + behind * upper
 
     rest = []
+    def put(k, i, value):
+        fields[k][i], halves[k][i] = value, 0.5 * value
+
     for i in range(-HALO, -2):
-        fields[0][i] = load(i)
+        put(0, i, load(i))
     for t in range(-4, rows + 6):
         active = [k for k in range(3) if reach[k][0] <= t - 3 * k <= reach[k][1]]
         if t + 2 < rows + HALO:
-            fields[0][t + 2] = load(t + 2)
+            put(0, t + 2, load(t + 2))
         for k in active:
             c = t - 3 * k
             if c == reach[k][0]:
-                f = fields[k]
                 for i in (c - 1, c, c + 1):
-                    steps[k][i] = f[i] - f[i - 1]
+                    steps[k][i] = halves[k][i] - halves[k][i - 1]
                 for i in (c - 1, c):
-                    slopes[k][i] = half_minmod(steps[k][i + 1], steps[k][i])
+                    slopes[k][i] = minmod(steps[k][i + 1], steps[k][i])
                 fluxes[k][c] = face([k], [c])
         at = [t - 3 * k for k in active]
         here = cat([fields[k][i] for k, i in zip(active, at)])
-        back = here - pltpu.roll(here, 1, 2)
+        half = cat([halves[k][i] for k, i in zip(active, at)])
+        back = half - pltpu.roll(half, 1, 2)
         new = cat(
-            [fields[k][i + 2] - fields[k][i + 1] for k, i in zip(active, at)]
+            [halves[k][i + 2] - halves[k][i + 1] for k, i in zip(active, at)]
         )
         last = cat([steps[k][i + 1] for k, i in zip(active, at)])
-        bend = half_minmod(pltpu.roll(back, LANES - 1, 2), back)
-        slope = half_minmod(new, last)
+        bend = minmod(pltpu.roll(back, LANES - 1, 2), back)
+        slope = minmod(new, last)
         for k, i, a_step, a_slope in zip(
             active, at, pieces(new, len(at)), pieces(slope, len(at))
         ):
@@ -433,9 +437,9 @@
         moved = here + (moved + (side - pltpu.roll(side, LANES - 1, 2)))
         for k, i, value in zip(active, at, pieces(moved, len(at))):
             if k == 0:
-                fields[1][i] = value
+                put(1, i, value)
             elif k == 1:
-                fields[2][i] = 0.75 * fields[0][i] + 0.25 * value
+                put(2, i, 0.75 * fields[0][i] + 0.25 * value)
             else:
                 value = 1.0 / 3.0 * fields[0][i] + 2.0 / 3.0 * value
                 value = value.reshape(GROUP, LANES)

time: 32.8 us -> 32.9 us (level)
  no operation moved by 1% of the time
where the time goes in v4:
time: 32.9 us; the launch traced here: 32.7 us
  Pallas kernels  23.8 us (72%)
  starting transfers between devices  5.47 us (17%)
  waiting for transfers between devices  2.6 us (8%)
  between operations  0.82 us (2%)
    pallas_call x1, Pallas kernels, network(): pl.pallas_call(functools.partial(network_kernel, sizes=sizes, levels=leve...  19.7 us
    ppermute x1, starting transfers between devices, shards(): got_a = lax.ppermute(pay_a, 'gx', outer)  5.47 us
    pallas_call x1, Pallas kernels, advect(): pl.pallas_call(functools.partial(advect_kernel, levels=levels, axis=axis)...  3.22 us
    ppermute x1, waiting for transfers between devices, shards(): got_a = lax.ppermute(pay_a, 'gx', outer)  2.6 us
    pallas_call x1, Pallas kernels, stage(): pl.pallas_call(stage_kernel, out_shape=jax.ShapeDtypeStruct((rows, *field...  0.96 us
  transfers between devices with their start and end apart: 2, of which 1 were waited for; matrix products, arithmetic and copies ran while one was open for 0% of the time, Pallas kernels for 3%

profile of v4, /device:TPU:0, one launch (start us, length us, event | category | flops | bytes accessed | tf_op | source)
XLA Modules:
  0.0 32.7 jit_solution(13339958959588687168)
XLA Ops:
  0.6 19.7 %column_network.1 = (f32[368,1024]{1,0:T(8,128)}, f32[128,64,128]{2,1,0:T(8,128)}, f32[6,64,128]{2,1,0:T(8,128)}, f32[6,64,128]{2,1,0:T(8,128)}) custom-call(s32[8,128]{1,0:T(8,128)} %bitcast.10, f32[480,128]{1,0:T(8,128)} %bitcast.9, f32[8,128]{1,0:T(8,128)} %refs_2_.1, f32[8,128]{1,0:T(8,128)} %refs_3_.1, f32[768]{0:T(1024)} %refs_4_.1, f32[640]{0:T(1024)} %refs_5_.1, ...), custom_call_target="tpu_custom_call" | custom-call | flops 9092202496 | bytes 14000000 | tf_op jit(solution)/shard_map/column_network/pallas_call | solution.py:273
  20.3 5.5 %collective-permute-start = (f32[6,64,128]{2,1,0:T(8,128)}, f32[6,64,128]{2,1,0:T(8,128)S(1)}, u32[]{:S(2)}, u32[]{:S(2)}) collective-permute-start(f32[6,64,128]{2,1,0:T(8,128)} %get-tuple-element.8), channel_id=1, source_target_pairs={{0,15},{1,2},{2,1},{3,4},{4,3},{5,6},{6,5},{7,8},{8,7},{9,10},{10,... | collective-permute-start | bytes 589832 | tf_op jit(solution)/shard_map/ppermute | solution.py:514
  25.8 0.0 collective-permute-start.1
  25.8 1.0 %stage_rows.1.field = f32[8,64,128]{2,1,0:T(8,128)S(1)} custom-call(f32[128,64,128]{2,1,0:T(8,128)} %get-tuple-element.7.field), custom_call_target="tpu_custom_call" | custom-call | bytes 4000000 | tf_op jit(solution)/shard_map/stage_rows/pallas_call | solution.py:464
  26.7 2.6 %collective-permute-done.got_a = f32[6,64,128]{2,1,0:T(8,128)S(1)} collective-permute-done((f32[6,64,128]{2,1,0:T(8,128)}, f32[6,64,128]{2,1,0:T(8,128)S(1)}, u32[]{:S(2)}, u32[]{:S(2)}) %collective-permute-start) | collective-permute-done | bytes 196640 | tf_op jit(solution)/shard_map/ppermute | solution.py:514
  29.3 0.0 collective-permute-done.1.got_b
  29.3 3.2 %advect_sections.1 = f32[480,128]{1,0:T(8,128)} custom-call(f32[8,64,128]{2,1,0:T(8,128)S(1)} %stage_rows.1.field, f32[6,64,128]{2,1,0:T(8,128)S(1)} %collective-permute-done.got_a, f32[6,64,128]{2,1,0:T(8,128)S(1)} %collective-permute-done.1.got_b), custom_call_target="tpu_custom_call" | custom-call | tf_op jit(solution)/shard_map/advect_sections/pallas_call | solution.py:481
Async XLA Ops:
  20.3 9.0 %collective-permute-start = (f32[6,64,128]{2,1,0:T(8,128)}, f32[6,64,128]{2,1,0:T(8,128)S(1)}, u32[]{:S(2)}, u32[]{:S(2)}) collective-permute-start(f32[6,64,128]{2,1,0:T(8,128)} %get-tuple-element.8), channel_id=1, source_target_pairs={{0,15},{1,2},{2,1},{3,4},{4,3},{5,6},{6,5},{7,8},{8,7},{9,10},{10,... | collective-permute-start | bytes 589832 | tf_op jit(solution)/shard_map/ppermute | solution.py:514
  25.8 3.6 %collective-permute-start.1 = (f32[6,64,128]{2,1,0:T(8,128)}, f32[6,64,128]{2,1,0:T(8,128)S(1)}, u32[]{:S(2)}, u32[]{:S(2)}) collective-permute-start(f32[6,64,128]{2,1,0:T(8,128)} %get-tuple-element.9), channel_id=1, source_target_pairs={{0,1},{1,0},{2,3},{3,2},{4,5},{5,4},{6,7},{7,6},{8,9},{9,8},{10,11... | collective-permute-start | bytes 589832 | tf_op jit(solution)/shard_map/ppermute | solution.py:515

commit v5 on v3

--- a/solution.py
+++ b/solution.py
@@ -315,11 +315,9 @@
     )(inverse, tracer, along, across, *biases, x, *weights)
 
 
-def half_minmod(first, second):
-    return 0.5 * (
-        jnp.maximum(jnp.minimum(first, second), 0.0)
-        + jnp.minimum(jnp.maximum(first, second), 0.0)
-    )
+def minmod(first, second):
+    high, low = jnp.maximum(second, 0.0), jnp.minimum(second, 0.0)
+    return jnp.maximum(jnp.minimum(first, high), low)
 
 
 def cat(values):
@@ -375,7 +373,7 @@
     base = pl.multiple_of(g * GROUP, GROUP)
     blocks = GROUP // 8
     keep = levels - (groups - 1) * GROUP
-    fields = [{}, {}, {}]
+    fields, halves, sides = [{}, {}, {}], [{}, {}, {}], [{}, {}, {}]
     steps, slopes, fluxes = [{}, {}, {}], [{}, {}, {}], [{}, {}, {}]
     reach = [(-4, rows + 3), (-2, rows + 1), (0, rows - 1)]
     shape = (blocks, 8, LANES)
@@ -396,51 +394,71 @@
         return ahead * lower + behind * upper
 
     rest = []
-    for i in range(-HALO, -2):
-        fields[0][i] = load(i)
-    for t in range(-4, rows + 6):
-        active = [k for k in range(3) if reach[k][0] <= t - 3 * k <= reach[k][1]]
-        if t + 2 < rows + HALO:
-            fields[0][t + 2] = load(t + 2)
-        for k in active:
-            c = t - 3 * k
-            if c == reach[k][0]:
-                f = fields[k]
-                for i in (c - 1, c, c + 1):
-                    steps[k][i] = f[i] - f[i - 1]
-                for i in (c - 1, c):
-                    slopes[k][i] = half_minmod(steps[k][i + 1], steps[k][i])
-                fluxes[k][c] = face([k], [c])
-        at = [t - 3 * k for k in active]
+    def put(k, i, value):
+        fields[k][i], halves[k][i] = value, 0.5 * value
+
+    def sideways(places):
+        at = [i for _, i in places]
+        here = cat([fields[k][i] for k, i in places])
+        half = cat([halves[k][i] for k, i in places])
+        back = half - pltpu.roll(half, 1, 2)
+        bend = minmod(pltpu.roll(back, LANES - 1, 2), back)
+        side = courant(2, at) * pltpu.roll(here + bend, 1, 2)
+        side = side + courant(3, at) * (here - bend)
+        side = side - pltpu.roll(side, LANES - 1, 2)
+        for (k, i), value in zip(places, pieces(side, len(at))):
+            sides[k][i] = value
+
+    for i in range(-HALO, 0):
+        put(0, i, load(i))
+    for t in range(-4, rows + 8):
+        active = [k for k in range(3) if reach[k][0] <= t - 4 * k <= reach[k][1]]
+        if t + 4 < rows + HALO:
+            put(0, t + 4, load(t + 4))
+        fresh = [k for k in active if t - 4 * k == reach[k][0]]
+        for k in fresh:
+            c = reach[k][0]
+            for i in (c - 1, c, c + 1):
+                steps[k][i] = halves[k][i] - halves[k][i - 1]
+            for i in (c - 1, c):
+                slopes[k][i] = minmod(steps[k][i + 1], steps[k][i])
+            fluxes[k][c] = face([k], [c])
+        if fresh:
+            sideways([(k, reach[k][0] + n) for k in fresh for n in (0, 1)])
+        at = [t - 4 * k for k in active]
         here = cat([fields[k][i] for k, i in zip(active, at)])
-        back = here - pltpu.roll(here, 1, 2)
         new = cat(
-            [fields[k][i + 2] - fields[k][i + 1] for k, i in zip(active, at)]
+            [halves[k][i + 2] - halves[k][i + 1] for k, i in zip(active, at)]
         )
         last = cat([steps[k][i + 1] for k, i in zip(active, at)])
-        bend = half_minmod(pltpu.roll(back, LANES - 1, 2), back)
-        slope = half_minmod(new, last)
+        slope = minmod(new, last)
         for k, i, a_step, a_slope in zip(
             active, at, pieces(new, len(at)), pieces(slope, len(at))
         ):
             steps[k][i + 2], slopes[k][i + 1] = a_step, a_slope
-        side = courant(2, at) * pltpu.roll(here + bend, 1, 2)
-        side = side + courant(3, at) * (here - bend)
         flux = face(active, [i + 1 for i in at])
         for k, i, a_flux in zip(active, at, pieces(flux, len(at))):
             fluxes[k][i + 1] = a_flux
         moved = cat([fluxes[k][i] for k, i in zip(active, at)]) - flux
-        moved = here + (moved + (side - pltpu.roll(side, LANES - 1, 2)))
+        moved = here + (moved + cat([sides[k][i] for k, i in zip(active, at)]))
         for k, i, value in zip(active, at, pieces(moved, len(at))):
             if k == 0:
-                fields[1][i] = value
+                put(1, i, value)
             elif k == 1:
-                fields[2][i] = 0.75 * fields[0][i] + 0.25 * value
+                put(2, i, 0.75 * fields[0][i] + 0.25 * value)
             else:
                 value = 1.0 / 3.0 * fields[0][i] + 2.0 / 3.0 * value
                 value = value.reshape(GROUP, LANES)
                 out[pl.ds(base * rows + i, keep, stride=rows), :] = value[:keep]
                 rest.append((i, value[keep:]))
+        ahead = [
+            (k, i + n)
+            for k, i in zip(active, at)
+            for n in (2, 3)
+            if (i - reach[k][0]) % 2 == 0 and i + n <= reach[k][1]
+        ]
+        if ahead:
+            sideways(ahead)
     if keep < GROUP:
 
         @pl.when(g < groups - 1)

time: 32.8 us -> 32.9 us (level)
  no operation moved by 1% of the time
where the time goes in v5:
time: 32.9 us; the launch traced here: 32.7 us
  Pallas kernels  23.8 us (72%)
  starting transfers between devices  5.48 us (17%)
  waiting for transfers between devices  2.6 us (8%)
  between operations  0.82 us (2%)
    pallas_call x1, Pallas kernels, network(): pl.pallas_call(functools.partial(network_kernel, sizes=sizes, levels=leve...  19.6 us
    ppermute x1, starting transfers between devices, shards(): got_a = lax.ppermute(pay_a, 'gx', outer)  5.48 us
    pallas_call x1, Pallas kernels, advect(): pl.pallas_call(functools.partial(advect_kernel, levels=levels, axis=axis)...  3.23 us
    ppermute x1, waiting for transfers between devices, shards(): got_a = lax.ppermute(pay_a, 'gx', outer)  2.6 us
    pallas_call x1, Pallas kernels, stage(): pl.pallas_call(stage_kernel, out_shape=jax.ShapeDtypeStruct((rows, *field...  0.96 us
  transfers between devices with their start and end apart: 2, of which 1 were waited for; matrix products, arithmetic and copies ran while one was open for 0% of the time, Pallas kernels for 3%

profile of v5, /device:TPU:0, one launch (start us, length us, event | category | flops | bytes accessed | tf_op | source)
XLA Modules:
  0.0 32.7 jit_solution(2615124975478476514)
XLA Ops:
  0.6 19.6 %column_network.1 = (f32[368,1024]{1,0:T(8,128)}, f32[128,64,128]{2,1,0:T(8,128)}, f32[6,64,128]{2,1,0:T(8,128)}, f32[6,64,128]{2,1,0:T(8,128)}) custom-call(s32[8,128]{1,0:T(8,128)} %bitcast.10, f32[480,128]{1,0:T(8,128)} %bitcast.9, f32[8,128]{1,0:T(8,128)} %refs_2_.1, f32[8,128]{1,0:T(8,128)} %refs_3_.1, f32[768]{0:T(1024)} %refs_4_.1, f32[640]{0:T(1024)} %refs_5_.1, ...), custom_call_target="tpu_custom_call" | custom-call | flops 9092202496 | bytes 14000000 | tf_op jit(solution)/shard_map/column_network/pallas_call | solution.py:270
  20.3 5.5 %collective-permute-start = (f32[6,64,128]{2,1,0:T(8,128)}, f32[6,64,128]{2,1,0:T(8,128)S(1)}, u32[]{:S(2)}, u32[]{:S(2)}) collective-permute-start(f32[6,64,128]{2,1,0:T(8,128)} %get-tuple-element.8), channel_id=1, source_target_pairs={{0,15},{1,2},{2,1},{3,4},{4,3},{5,6},{6,5},{7,8},{8,7},{9,10},{10,... | collective-permute-start | bytes 589832 | tf_op jit(solution)/shard_map/ppermute | solution.py:528
  25.8 0.0 collective-permute-start.1
  25.8 1.0 %stage_rows.1.field = f32[8,64,128]{2,1,0:T(8,128)S(1)} custom-call(f32[128,64,128]{2,1,0:T(8,128)} %get-tuple-element.7.field), custom_call_target="tpu_custom_call" | custom-call | bytes 4000000 | tf_op jit(solution)/shard_map/stage_rows/pallas_call | solution.py:478
  26.7 2.6 %collective-permute-done.got_a = f32[6,64,128]{2,1,0:T(8,128)S(1)} collective-permute-done((f32[6,64,128]{2,1,0:T(8,128)}, f32[6,64,128]{2,1,0:T(8,128)S(1)}, u32[]{:S(2)}, u32[]{:S(2)}) %collective-permute-start) | collective-permute-done | bytes 196640 | tf_op jit(solution)/shard_map/ppermute | solution.py:528
  29.3 0.0 collective-permute-done.1.got_b
  29.3 3.2 %advect_sections.1 = f32[480,128]{1,0:T(8,128)} custom-call(f32[8,64,128]{2,1,0:T(8,128)S(1)} %stage_rows.1.field, f32[6,64,128]{2,1,0:T(8,128)S(1)} %collective-permute-done.got_a, f32[6,64,128]{2,1,0:T(8,128)S(1)} %collective-permute-done.1.got_b), custom_call_target="tpu_custom_call" | custom-call | tf_op jit(solution)/shard_map/advect_sections/pallas_call | solution.py:495
Async XLA Ops:
  20.3 9.0 %collective-permute-start = (f32[6,64,128]{2,1,0:T(8,128)}, f32[6,64,128]{2,1,0:T(8,128)S(1)}, u32[]{:S(2)}, u32[]{:S(2)}) collective-permute-start(f32[6,64,128]{2,1,0:T(8,128)} %get-tuple-element.8), channel_id=1, source_target_pairs={{0,15},{1,2},{2,1},{3,4},{4,3},{5,6},{6,5},{7,8},{8,7},{9,10},{10,... | collective-permute-start | bytes 589832 | tf_op jit(solution)/shard_map/ppermute | solution.py:528
  25.8 3.6 %collective-permute-start.1 = (f32[6,64,128]{2,1,0:T(8,128)}, f32[6,64,128]{2,1,0:T(8,128)S(1)}, u32[]{:S(2)}, u32[]{:S(2)}) collective-permute-start(f32[6,64,128]{2,1,0:T(8,128)} %get-tuple-element.9), channel_id=1, source_target_pairs={{0,1},{1,0},{2,3},{3,2},{4,5},{5,4},{6,7},{7,6},{8,9},{9,8},{10,11... | collective-permute-start | bytes 589832 | tf_op jit(solution)/shard_map/ppermute | solution.py:529

commit v6 on v3

--- a/solution.py
+++ b/solution.py
@@ -17,7 +17,7 @@
 SILU_DIP = 0.28
 TOP = 440.0
 INPUT_SCALE = 72.0
-MIXED = (0, 1, 3, 4)
+MIXED = (0, 1, 2, 3, 4, 5)
 WEIGHT_STEP = 2.0**10
 LOW_STEP = 2.0**8
 NETWORK_VMEM = 60_000_000

time: 32.8 us -> 32.1 us (0.979)
  Pallas kernels: 23.7 us -> 23.1 us
    pallas_call x1, Pallas kernels: 19.6 us -> 19 us  [network(): pl.pallas_call(functools.partial(network_kernel, sizes=sizes, levels=leve...]
where the time goes in v6:
time: 32.1 us; the launch traced here: 32 us
  Pallas kernels  23.1 us (72%)
  starting transfers between devices  5.49 us (17%)
  waiting for transfers between devices  2.6 us (8%)
  between operations  0.82 us (3%)
    pallas_call x1, Pallas kernels, network(): pl.pallas_call(functools.partial(network_kernel, sizes=sizes, levels=leve...  19 us
    ppermute x1, starting transfers between devices, shards(): got_a = lax.ppermute(pay_a, 'gx', outer)  5.48 us
    pallas_call x1, Pallas kernels, advect(): pl.pallas_call(functools.partial(advect_kernel, levels=levels, axis=axis)...  3.13 us
    ppermute x1, waiting for transfers between devices, shards(): got_a = lax.ppermute(pay_a, 'gx', outer)  2.6 us
    pallas_call x1, Pallas kernels, stage(): pl.pallas_call(stage_kernel, out_shape=jax.ShapeDtypeStruct((rows, *field...  0.96 us
  transfers between devices with their start and end apart: 2, of which 1 were waited for; matrix products, arithmetic and copies ran while one was open for 0% of the time, Pallas kernels for 3%

profile of v6, /device:TPU:0, one launch (start us, length us, event | category | flops | bytes accessed | tf_op | source)
XLA Modules:
  0.0 32.0 jit_solution(16147459786870172079)
XLA Ops:
  0.6 19.0 %column_network.1 = (f32[368,1024]{1,0:T(8,128)}, f32[128,64,128]{2,1,0:T(8,128)}, f32[6,64,128]{2,1,0:T(8,128)}, f32[6,64,128]{2,1,0:T(8,128)}) custom-call(s32[8,128]{1,0:T(8,128)} %bitcast.10, f32[480,128]{1,0:T(8,128)} %bitcast.9, f32[8,128]{1,0:T(8,128)} %refs_2_.1, f32[8,128]{1,0:T(8,128)} %refs_3_.1, f32[768]{0:T(1024)} %refs_4_.1, f32[640]{0:T(1024)} %refs_5_.1, ...), custom_call_target="tpu_custom_call" | custom-call | flops 9092202496 | bytes 14000000 | tf_op jit(solution)/shard_map/column_network/pallas_call | solution.py:270
  19.6 5.5 %collective-permute-start = (f32[6,64,128]{2,1,0:T(8,128)}, f32[6,64,128]{2,1,0:T(8,128)S(1)}, u32[]{:S(2)}, u32[]{:S(2)}) collective-permute-start(f32[6,64,128]{2,1,0:T(8,128)} %get-tuple-element.8), channel_id=1, source_target_pairs={{0,15},{1,2},{2,1},{3,4},{4,3},{5,6},{6,5},{7,8},{8,7},{9,10},{10,... | collective-permute-start | bytes 589832 | tf_op jit(solution)/shard_map/ppermute | solution.py:510
  25.1 0.0 collective-permute-start.1
  25.1 1.0 %stage_rows.1.field = f32[8,64,128]{2,1,0:T(8,128)S(1)} custom-call(f32[128,64,128]{2,1,0:T(8,128)} %get-tuple-element.7.field), custom_call_target="tpu_custom_call" | custom-call | bytes 4000000 | tf_op jit(solution)/shard_map/stage_rows/pallas_call | solution.py:460
  26.1 2.6 %collective-permute-done.got_a = f32[6,64,128]{2,1,0:T(8,128)S(1)} collective-permute-done((f32[6,64,128]{2,1,0:T(8,128)}, f32[6,64,128]{2,1,0:T(8,128)S(1)}, u32[]{:S(2)}, u32[]{:S(2)}) %collective-permute-start) | collective-permute-done | bytes 196640 | tf_op jit(solution)/shard_map/ppermute | solution.py:510
  28.7 0.0 collective-permute-done.1.got_b
  28.7 3.1 %advect_sections.1 = f32[480,128]{1,0:T(8,128)} custom-call(f32[8,64,128]{2,1,0:T(8,128)S(1)} %stage_rows.1.field, f32[6,64,128]{2,1,0:T(8,128)S(1)} %collective-permute-done.got_a, f32[6,64,128]{2,1,0:T(8,128)S(1)} %collective-permute-done.1.got_b), custom_call_target="tpu_custom_call" | custom-call | tf_op jit(solution)/shard_map/advect_sections/pallas_call | solution.py:477
Async XLA Ops:
  19.6 9.0 %collective-permute-start = (f32[6,64,128]{2,1,0:T(8,128)}, f32[6,64,128]{2,1,0:T(8,128)S(1)}, u32[]{:S(2)}, u32[]{:S(2)}) collective-permute-start(f32[6,64,128]{2,1,0:T(8,128)} %get-tuple-element.8), channel_id=1, source_target_pairs={{0,15},{1,2},{2,1},{3,4},{4,3},{5,6},{6,5},{7,8},{8,7},{9,10},{10,... | collective-permute-start | bytes 589832 | tf_op jit(solution)/shard_map/ppermute | solution.py:510
  25.1 3.6 %collective-permute-start.1 = (f32[6,64,128]{2,1,0:T(8,128)}, f32[6,64,128]{2,1,0:T(8,128)S(1)}, u32[]{:S(2)}, u32[]{:S(2)}) collective-permute-start(f32[6,64,128]{2,1,0:T(8,128)} %get-tuple-element.9), channel_id=1, source_target_pairs={{0,1},{1,0},{2,3},{3,2},{4,5},{5,4},{6,7},{7,6},{8,9},{9,8},{10,11... | collective-permute-start | bytes 589832 | tf_op jit(solution)/shard_map/ppermute | solution.py:511
